TPU v7x, 128 devices: a whole 4x4x4 slice. The times are simulated.
128 devices in a mesh: pack: 8 (over z, core), seq: 16 (over x, y).
Axes of the slice: x: 4, y: 4, z: 4, core: 2. Of those that a mesh axis runs over, the one named last changes fastest.
Arguments:
- inputs: bfloat16 [8, 8192, 512], P('pack', 'seq'), may hold values from -6 to 6
- w_query: bfloat16 [512, 512], replicated, may hold values from -0.25 to 0.25
- w_key: bfloat16 [512, 512], replicated, may hold values from -0.25 to 0.25
- w_value: bfloat16 [512, 512], replicated, may hold values from -0.25 to 0.25
- w_output: bfloat16 [512, 512], replicated, may hold values from -6 to 6
- w_up: bfloat16 [512, 2048], replicated, may hold values from -0.25 to 0.25
- w_down: bfloat16 [2048, 512], replicated, may hold values from -0.125 to 0.125
- gain_attn: float32 [512], replicated, may hold values from 0.5 to 1.5
- gain_ffn: float32 [512], replicated, may hold values from 0.5 to 1.5
- random_features: bfloat16 [8, 64, 256], replicated, may hold values from -4 to 4
- doc_ids: int32 [8, 8192], P('pack', 'seq'), may hold values from 0 to 9, as said below
- live_rows: int32 [8, 8192], P('pack', 'seq'), may hold values from 0 to 1, as said below
- cotangent: bfloat16 [8, 8192, 512], P('pack', 'seq'), may hold values from -6 to 6
Outputs:
- outputs: bfloat16 [8, 8192, 512], P('pack', 'seq')
- grad_inputs: bfloat16 [8, 8192, 512], P('pack', 'seq')
- grad_w_query: float32 [512, 512], replicated
- grad_w_key: float32 [512, 512], replicated
- grad_w_value: float32 [512, 512], replicated
- grad_w_output: float32 [512, 512], replicated
- grad_w_up: float32 [512, 2048], replicated
- grad_w_down: float32 [2048, 512], replicated
- grad_gain_attn: float32 [512], replicated
- grad_gain_ffn: float32 [512], replicated
Inputs may be any that keep to these rules, and one draw needn't show every extreme that they name: `doc_ids`: document numbers never fall along a pack, and each of the 10 documents of a pack has at least one row. `live_rows`: the first row of every document is live.
All inputs are finite; a program needn't handle non-finite values.
Results may differ from a plain program's by a relative error of at most 0.025.
Values sent between devices are 32-bit elements; how exact they have to be, the bound alone decides.
A program may use at most 128 MiB of HBM per device.

v0:
```python
import math

import jax
import jax.numpy as jnp
from jax import lax
from jax.sharding import PartitionSpec as P

SEGS = 10


epsilon = 1e-05
highest_precision_flag = lax.Precision.HIGHEST


def layer_norm(values, gain_vec):
    average = jnp.mean(values, axis=-1, keepdims=True)
    centred = values - average
    spread = jnp.mean(centred * centred, axis=-1, keepdims=True)
    return centred * lax.rsqrt(spread + epsilon) * gain_vec


def feature_exp(project, head_float):
    square = jnp.sum(head_float * head_float, axis=-1, keepdims=True)
    factor = head_float.shape[-1] ** (-0.25)
    return jnp.exp(factor * project - 0.5 * factor * factor * square) / math.sqrt(project.shape[-1])


def contract(left_side, right_side, left_dim, right_dim):
    return lax.dot_general(
        left_side,
        right_side,
        (((left_dim,), (right_dim,)), ((), ())),
        preferred_element_type=jnp.float32,
    )


def settle(local_part, arrived):
    return local_part + (arrived - local_part)


def per_device(
    inputs,
    w_query,
    w_key,
    w_value,
    w_output,
    w_up,
    w_down,
    gain_attn,
    gain_ffn,
    random_features,
    doc_ids,
    live_rows,
    cotangent,
):
    rows = inputs[0].astype(jnp.float32)
    seq_rows, model_width = rows.shape
    head_count, head_size, feat_count = random_features.shape
    doc_rows = doc_ids[0]
    onehot = (doc_rows[:, None] == jnp.arange(SEGS, dtype=jnp.int32)[None, :]).astype(jnp.bfloat16)
    onehot_float = onehot.astype(jnp.float32)
    onehot_mask = onehot[:, :, None, None]
    live_mask = live_rows[0].astype(jnp.float32)[:, None, None]
    normed_float, norm_pull_attn = jax.vjp(layer_norm, rows, gain_attn)
    normed = normed_float.astype(jnp.bfloat16)
    query_flat = jnp.dot(normed, w_query, preferred_element_type=jnp.float32).astype(jnp.bfloat16)
    key_flat = jnp.dot(normed, w_key, preferred_element_type=jnp.float32).astype(jnp.bfloat16)
    value_flat = jnp.dot(normed, w_value, preferred_element_type=jnp.float32).astype(jnp.bfloat16)
    query_heads = query_flat.reshape(seq_rows, head_count, head_size)
    key_heads = key_flat.reshape(seq_rows, head_count, head_size)
    value_head_rows = value_flat.reshape(seq_rows, head_count, head_size)

    def feature_pass(head_rows):
        project = jnp.einsum(
            "thd,hdm->thm", head_rows, random_features, preferred_element_type=jnp.float32
        )
        return jax.vjp(feature_exp, project, head_rows.astype(jnp.float32))

    phi_query_float, query_pull = feature_pass(query_heads)
    phi_key_float, key_pull = feature_pass(key_heads)
    phi_query = phi_query_float.astype(jnp.bfloat16)
    phi_key = (phi_key_float * live_mask).astype(jnp.bfloat16)
    masked_key = phi_key[:, None, :, :] * onehot_mask
    local_summary = jnp.einsum(
        "tshm,thd->shmd", masked_key, value_head_rows, preferred_element_type=jnp.float32
    )
    local_totals = jnp.einsum("ts,thm->shm", onehot, phi_key, preferred_element_type=jnp.float32)
    summed_docs, summed_tots = lax.psum((local_summary, local_totals), "seq")
    summary = settle(local_summary, summed_docs)
    totals = settle(local_totals, summed_tots)
    summary_low = summary.astype(jnp.bfloat16)
    masked_query = phi_query[:, None, :, :] * onehot_mask
    numerator = jnp.einsum(
        "tshm,shmd->thd", masked_query, summary_low, preferred_element_type=jnp.float32
    )
    row_totals = jnp.einsum("ts,shm->thm", onehot_float, totals, precision=highest_precision_flag)
    denominator = jnp.sum(phi_query.astype(jnp.float32) * row_totals, axis=-1)
    attended = (
        (numerator / denominator[:, :, None]).reshape(seq_rows, model_width).astype(jnp.bfloat16)
    )
    middle = rows + jnp.dot(attended, w_output, preferred_element_type=jnp.float32)
    hidden_float, norm_pull_ffn = jax.vjp(layer_norm, middle, gain_ffn)
    hidden = hidden_float.astype(jnp.bfloat16)
    upward_projection = jnp.dot(hidden, w_up, preferred_element_type=jnp.float32)
    activated_float, gelu_pull = jax.vjp(jax.nn.gelu, upward_projection)
    activated = activated_float.astype(jnp.bfloat16)
    outputs = middle + jnp.dot(activated, w_down, preferred_element_type=jnp.float32)
    output_gradient_rows = cotangent[0]
    grad_activated = contract(output_gradient_rows, w_down, 1, 1).astype(jnp.bfloat16)
    grad_w_down = contract(activated, output_gradient_rows, 0, 0)
    (grad_upward_float,) = gelu_pull(grad_activated.astype(jnp.float32))
    grad_upward = grad_upward_float.astype(jnp.bfloat16)
    grad_w_up = contract(hidden, grad_upward, 0, 0)
    grad_hidden = contract(grad_upward, w_up, 1, 1).astype(jnp.bfloat16)
    grad_middle_norm, grad_gain_ffn = norm_pull_ffn(grad_hidden.astype(jnp.float32))
    grad_middle = output_gradient_rows.astype(jnp.float32) + grad_middle_norm
    grad_branch = grad_middle.astype(jnp.bfloat16)
    grad_w_output = contract(attended, grad_branch, 0, 0)
    grad_attended = contract(grad_branch, w_output, 1, 1).astype(jnp.bfloat16).astype(jnp.float32)
    grad_attended = grad_attended.reshape(seq_rows, head_count, head_size)
    grad_numerator = (grad_attended / denominator[:, :, None]).astype(jnp.bfloat16)
    grad_denominator = -jnp.sum(grad_attended * numerator, axis=-1) / (denominator * denominator)
    masked_grad = grad_numerator[:, None, :, :] * onehot_mask
    grad_phi_query = jnp.einsum(
        "tshd,shmd->thm", masked_grad, summary_low, preferred_element_type=jnp.float32
    )
    grad_phi_query = (grad_phi_query + grad_denominator[:, :, None] * row_totals).astype(
        jnp.bfloat16
    )
    local_grad_summary = jnp.einsum(
        "tshm,thd->shmd", masked_query, grad_numerator, preferred_element_type=jnp.float32
    )
    local_grad_totals = jnp.einsum(
        "ts,thm->shm",
        onehot_float,
        phi_query.astype(jnp.float32) * grad_denominator[:, :, None],
        precision=highest_precision_flag,
    )
    summed_grad_docs, summed_grad_tots = lax.psum((local_grad_summary, local_grad_totals), "seq")
    grad_summary = settle(local_grad_summary, summed_grad_docs)
    grad_totals = settle(local_grad_totals, summed_grad_tots)
    grad_summary_low = grad_summary.astype(jnp.bfloat16)
    masked_value = value_head_rows[:, None, :, :] * onehot_mask
    grad_phi_key = jnp.einsum(
        "tshd,shmd->thm", masked_value, grad_summary_low, preferred_element_type=jnp.float32
    )
    grad_phi_key = grad_phi_key + jnp.einsum(
        "ts,shm->thm", onehot_float, grad_totals, precision=highest_precision_flag
    )
    grad_phi_key = grad_phi_key.astype(jnp.bfloat16).astype(jnp.float32) * live_mask
    grad_value = jnp.einsum(
        "tshm,shmd->thd", masked_key, grad_summary_low, preferred_element_type=jnp.float32
    ).astype(jnp.bfloat16)

    def heads_back(pull, grad_phi):
        grad_project, grad_square = pull(grad_phi)
        through = jnp.einsum(
            "thm,hdm->thd",
            grad_project.astype(jnp.bfloat16),
            random_features,
            preferred_element_type=jnp.float32,
        )
        return (through + grad_square).astype(jnp.bfloat16)

    grad_query = heads_back(query_pull, grad_phi_query.astype(jnp.float32)).reshape(
        seq_rows, model_width
    )
    grad_key = heads_back(key_pull, grad_phi_key).reshape(seq_rows, model_width)
    grad_value = grad_value.reshape(seq_rows, model_width)
    grad_normed = (
        contract(grad_query, w_query, 1, 1)
        + contract(grad_key, w_key, 1, 1)
        + contract(grad_value, w_value, 1, 1)
    )
    grad_normed = grad_normed.astype(jnp.bfloat16)
    grad_w_query = contract(normed, grad_query, 0, 0)
    grad_w_key = contract(normed, grad_key, 0, 0)
    grad_w_value = contract(normed, grad_value, 0, 0)
    grad_rows_norm, grad_gain_attn = norm_pull_attn(grad_normed.astype(jnp.float32))
    grad_inputs = grad_middle + grad_rows_norm
    summed = lax.psum(
        (
            grad_w_query,
            grad_w_key,
            grad_w_value,
            grad_w_output,
            grad_w_up,
            grad_w_down,
            grad_gain_attn,
            grad_gain_ffn,
        ),
        ("pack", "seq"),
    )
    return (
        outputs[None].astype(jnp.bfloat16),
        grad_inputs[None].astype(jnp.bfloat16),
        summed[0],
        summed[1],
        summed[2],
        summed[3],
        summed[4],
        summed[5],
        summed[6],
        summed[7],
    )


def solution(mesh):
    return jax.shard_map(
        per_device,
        mesh=mesh,
        in_specs=(
            P("pack", "seq", None),
            P(),
            P(),
            P(),
            P(),
            P(),
            P(),
            P(),
            P(),
            P(),
            P("pack", "seq"),
            P("pack", "seq"),
            P("pack", "seq", None),
        ),
        out_specs=(
            P("pack", "seq", None),
            P("pack", "seq", None),
            P(),
            P(),
            P(),
            P(),
            P(),
            P(),
            P(),
            P(),
        ),
        check_vma=False,
    )
```

profile of v0, /device:TPU:1, one launch (start us, length us, event | category | flops | bytes accessed | tf_op | source)
XLA Modules:
  0.0 520.4 jit_solution(8304739650043268187)
XLA Ops:
  7.3 1.4 copy.23
  9.7 1.6 fusion.85
  12.1 3.0 multiply_convert_fusion.4
  15.1 1.3 copy-done.6
  16.4 1.3 fusion.112
  17.8 3.9 copy.24
  23.0 7.6 %fusion.42 = f32[10,8,256,64]{2,3,0,1:T(8,128)} fusion(bf16[512,8,64,1]{0,2,3,1:T(8,128)(2,1)S(1)} %bitcast.223, bf16[512,10]{0,1:T(8,128)(2,1)S(1)} %fusion.108, bf16[512,8,256]{2,0,1:T(8,128)(2,1)} %copy.24), kind=kOutput, calls=%fused_computation.62 | convolution fusion | flops 1384120320 | bytes 7874560 | tf_op jit(solution)/shard_map/tshm,thd->shmd/dot_general | solution.py:84
  30.7 1.0 copy-done.33
  31.6 1.0 copy.28
  32.6 1.6 fusion.87
  34.3 2.8 fusion.137
  37.0 110.9 %all-reduce.12.cloned.1.call-done = (f32[10,8,256,64]{2,3,0,1:T(8,128)}, f32[10,8,256]{2,0,1:T(8,128)}) async-done(((f32[10,8,256,64]{2,3,0,1:T(8,128)}, f32[10,8,256]{2,0,1:T(8,128)}), (f32[10,8,256,64]{2,3,0,1:T(8,128)}, f32[10,8,256]{2,0,1:T(8,128)})) %all-reduce.12.cloned.1.call-update) | async-done | bytes 5324816 | tf_op jit(solution)/shard_map/psum | solution.py:88
  147.9 7.0 %fusion.16 = bf16[10,8,256,64]{2,3,0,1:T(8,128)(2,1)} fusion(f32[10,8,256,64]{2,3,0,1:T(8,128)} %fusion.42, f32[10,8,256,64]{2,3,0,1:T(8,128)} %get-tuple-element.34), kind=kLoop, calls=%fused_computation.24 | loop fusion | flops 3932160 | bytes 13107200 | tf_op jit(solution)/shard_map/convert_element_type | solution.py:91
  154.9 5.4 %fusion.22 = (f32[512,8]{0,1:T(8,128)S(1)}, bf16[512,8,256]{0,2,1:T(8,128)(2,1)}, f32[512,8,256]{0,2,1:T(8,128)}) fusion(f32[512,8]{0,1:T(8,128)S(1)} %broadcast_multiply_fusion, f32[8,512,256]{1,2,0:T(8,128)S(1)} %copy-done.8, f32[10,8,256]{2,0,1:T(8,128)S(1)} %copy-done.30, f32[10,8,256]{2,0,1:T(8,128)S(1)} %copy-done.48, s32[512]{0:T(512)S(1)} %bitcast.217), kind=kOutput, calls=%fused_computation.30 | convolution fusion | flops 133211136 | bytes 10684416 | tf_op jit(solution)/shard_map/ts,shm->thm/dot_general | solution.py:96
  160.3 4.1 copy.25
  164.4 8.8 %divide_convert_fusion = (bf16[512,8,64]{0,2,1:T(8,128)(2,1)S(1)}, f32[512,8,64]{0,2,1:T(8,128)S(1)}) fusion(f32[512,8]{0,1:T(8,128)S(1)} %get-tuple-element.36, bf16[10,8,256,64]{2,3,0,1:T(8,128)(2,1)} %fusion.16, bf16[512,8,256]{2,0,1:T(8,128)(2,1)} %copy.25, bf16[512,10]{0,1:T(8,128)(2,1)S(1)} %fusion.108), kind=kOutput, calls=%fused_computation.134 | convolution fusion | flops 1353187328 | bytes 6318080 | tf_op jit(solution)/shard_map/tshm,shmd->thd/dot_general | solution.py:93
  174.0 1.4 fusion.124
  175.5 3.5 fusion.26
  179.1 1.3 fusion.84
  183.1 2.9 fusion.23
  185.9 6.1 %fusion.45 = f32[10,8,256,64]{2,3,0,1:T(8,128)} fusion(bf16[512,8,256]{2,0,1:T(8,128)(2,1)S(1)} %copy-done.23, bf16[512,10]{0,1:T(8,128)(2,1)S(1)} %fusion.108, bf16[512,8,64]{0,2,1:T(8,128)(2,1)S(1)} %fusion.91), kind=kOutput, calls=%fused_computation.63 | convolution fusion | flops 1384120320 | bytes 7874560 | tf_op jit(solution)/shard_map/tshm,thd->shmd/dot_general | solution.py:130
  193.1 6.0 %fusion.136 = (f32[512,8]{0,1:T(8,128)S(1)}, f32[512,8,256]{0,2,1:T(8,128)S(1)}) fusion(f32[512,8]{0,1:T(8,128)S(1)} %broadcast_multiply_fusion, f32[8,512,256]{1,2,0:T(8,128)} %fusion.137, f32[512,8,256]{0,2,1:T(8,128)} %get-tuple-element.44, f32[512,8]{0,1:T(8,128)S(1)} %multiply_divide_fusion, bf16[10,8,256,64]{2,3,0,1:T(8,128)(2,1)} %fusion.16, ...), kind=kOutput, calls=%fused_computation.180 | convolution fusion | flops 1354231808 | bytes 15788032 | tf_op jit(solution)/shard_map/tshd,shmd->thm/dot_general | solution.py:124
  199.2 1.4 fusion.138
  201.2 1.5 fusion.129
  202.7 3.4 fusion.123
  206.0 3.8 fusion.101
  209.8 96.1 %all-reduce.10.cloned.1.call-done = (f32[10,8,256,64]{2,3,0,1:T(8,128)}, f32[10,8,256]{2,0,1:T(8,128)}) async-done(((f32[10,8,256,64]{2,3,0,1:T(8,128)}, f32[10,8,256]{2,0,1:T(8,128)}), (f32[10,8,256,64]{2,3,0,1:T(8,128)}, f32[10,8,256]{2,0,1:T(8,128)})) %all-reduce.10.cloned.1.call-update) | async-done | bytes 5324816 | tf_op jit(solution)/shard_map/psum | solution.py:139
  305.9 5.5 %fusion.17 = bf16[10,8,256,64]{2,3,0,1:T(8,128)(2,1)S(1)} fusion(f32[10,8,256,64]{2,3,0,1:T(8,128)} %fusion.45, f32[10,8,256,64]{2,3,0,1:T(8,128)} %get-tuple-element.32), kind=kLoop, calls=%fused_computation.25 | loop fusion | flops 3932160 | bytes 13107200 | tf_op jit(solution)/shard_map/convert_element_type | solution.py:142
  311.4 7.0 %fusion.71 = bf16[8,64,512]{2,1,0:T(8,128)(2,1)S(1)} fusion(bf16[10,8,256,64]{2,3,0,1:T(8,128)(2,1)S(1)} %fusion.17, bf16[512,10]{0,1:T(8,128)(2,1)S(1)} %fusion.108, bf16[512,8,256]{2,0,1:T(8,128)(2,1)S(1)} %copy-done.22), kind=kOutput, calls=%fused_computation.100 | convolution fusion | flops 1352925184 | bytes 5253120 | tf_op jit(solution)/shard_map/tshm,shmd->thd/dot_general | solution.py:151
  318.5 1.8 fusion.18
  320.8 3.2 fusion.53
  324.0 1.6 fusion.76
  326.4 1.5 fusion.127
  327.9 1.5 fusion.125
  329.4 4.8 fusion.81
  334.2 1.0 copy.32
  335.7 1.7 convolution_add_fusion.1
  338.6 1.6 fusion.105
  340.2 2.0 copy.33
  342.2 65.7 %all-reduce = (f32[512]{0:T(512)}, f32[512]{0:T(512)}) all-reduce(f32[512]{0:T(512)S(1)} %get-tuple-element.22, f32[512]{0:T(512)S(1)} %get-tuple-element.20), channel_id=1, replica_groups=mesh['pack'=8,'seq'=16] {'pack','seq'}, use_global_device_ids=true, to_apply=%region_25.0 | all-reduce | flops 1024 | bytes 8192 | tf_op jit(solution)/shard_map/psum | solution.py:181
  407.9 93.1 %all-reduce.8.cloned.1.call-done = (f32[512,512]{1,0:T(8,128)}, f32[512,512]{1,0:T(8,128)}, f32[512,512]{1,0:T(8,128)}, f32[512,512]{1,0:T(8,128)}, f32[512,2048]{1,0:T(8,128)}, /*index=5*/f32[2048,512]{1,0:T(8,128)}) async-done(((f32[512,512]{1,0:T(8,128)}, f32[512,512]{1,0:T(8,128)}, f32[512,512]{1,0:T(8,128)}, f32[512,512]{1,0:T(8,128)}, f32[512,2048]{1,0:T(8,128)}, /*index=5*/f32[2048,512]{1,0:T(8,128)}), ...) | async-done | bytes 12582928 | tf_op jit(solution)/shard_map/psum | solution.py:181
  501.0 2.4 copy.55
  503.4 2.4 copy.56
  505.8 1.0 copy.57
  506.8 1.0 copy.58
  507.7 2.1 copy.59
  509.9 1.6 copy-done.17
  511.4 2.0 copy.60
  (140 shorter events, 11.2 us)
Async XLA Ops:
  7.2 166.8 %copy-start = (bf16[512,2048]{1,0:T(8,128)(2,1)S(1)}, bf16[512,2048]{1,0:T(8,128)(2,1)}, u32[]{:S(2)}) copy-start(bf16[512,2048]{1,0:T(8,128)(2,1)} %param.18) | copy-start | bytes 6291460
  7.2 4.1 copy-start.49
  7.2 4.9 copy-start.19
  7.2 140.7 %all-reduce.12.cloned.1.call-start = ((), (), s32[]{:S(2)}) async-start(), calls=%async_computation.2 | async-start | bytes 10747904 | tf_op jit(solution)/shard_map/psum | solution.py:88
  8.7 24.0 %copy-start.2 = (bf16[1,512,512]{1,2,0:T(8,128)(2,1)}, bf16[1,512,512]{1,2,0:T(8,128)(2,1)S(1)}, u32[]{:S(2)}) copy-start(bf16[1,512,512]{1,2,0:T(8,128)(2,1)S(1)} %copy.23) | copy-start | bytes 1572868
  15.1 6.5 %copy-start.39 = (bf16[512,512]{1,0:T(8,128)(2,1)S(1)}, bf16[512,512]{1,0:T(8,128)(2,1)}, u32[]{:S(2)}) copy-start(bf16[512,512]{1,0:T(8,128)(2,1)} %param.16) | copy-start | bytes 1572868
  15.1 6.5 %copy-start.50 = (f32[512]{0:T(512)S(1)}, f32[512]{0:T(512)}, u32[]{:S(2)}) copy-start(f32[512]{0:T(512)} %param.20) | copy-start | bytes 6148
  30.6 275.3 %all-reduce.10.cloned.1.call-start = ((), (), s32[]{:S(2)}) async-start(), calls=%async_computation.1 | async-start | bytes 10747904 | tf_op jit(solution)/shard_map/psum | solution.py:139
  34.2 120.7 %copy-start.25 = (bf16[512,512]{0,1:T(8,128)(2,1)}, bf16[512,512]{0,1:T(8,128)(2,1)S(1)}, u32[]{:S(2)}) copy-start(bf16[512,512]{0,1:T(8,128)(2,1)S(1)} %get-tuple-element.43) | copy-start | bytes 1572868
  147.9 7.0 %copy-start.8 = (f32[8,512,256]{1,2,0:T(8,128)S(1)}, f32[8,512,256]{1,2,0:T(8,128)}, u32[]{:S(2)}) copy-start(f32[8,512,256]{1,2,0:T(8,128)} %fusion.137) | copy-start | bytes 12582916
  147.9 7.0 %copy-start.30 = (f32[10,8,256]{2,0,1:T(8,128)S(1)}, f32[10,8,256]{2,0,1:T(8,128)}, u32[]{:S(2)}) copy-start(f32[10,8,256]{2,0,1:T(8,128)} %fusion.112) | copy-start | bytes 245764
  147.9 7.0 %copy-start.48 = (f32[10,8,256]{2,0,1:T(8,128)S(1)}, f32[10,8,256]{2,0,1:T(8,128)}, u32[]{:S(2)}) copy-start(f32[10,8,256]{2,0,1:T(8,128)} %get-tuple-element.35) | copy-start | bytes 245764
  164.4 8.9 %copy-start.3 = (bf16[1,512,512]{1,2,0:T(8,128)(2,1)S(1)}, bf16[1,512,512]{1,2,0:T(8,128)(2,1)}, u32[]{:S(2)}) copy-start(bf16[1,512,512]{1,2,0:T(8,128)(2,1)} %copy-done.2) | copy-start | bytes 1572868
  164.4 8.9 %copy-start.24 = (bf16[512,512]{1,0:T(8,128)(2,1)S(1)}, bf16[512,512]{1,0:T(8,128)(2,1)}, u32[]{:S(2)}) copy-start(bf16[512,512]{1,0:T(8,128)(2,1)} %param.17) | copy-start | bytes 1572868
  164.4 9.6 %copy-start.46 = (f32[512]{0:T(512)S(1)}, f32[512]{0:T(512)}, u32[]{:S(2)}) copy-start(f32[512]{0:T(512)} %param.21) | copy-start | bytes 6148
  173.2 2.2 copy-start.27
  173.8 1.8 copy-start.51
  175.5 3.5 copy-start.15
  179.1 2.0 copy-start.20
  179.1 2.1 copy-start.13
  180.4 2.6 copy-start.5
  181.2 4.7 copy-start.23
  183.0 2.9 copy-start.36
  192.1 308.9 %all-reduce.8.cloned.1.call-start = ((), (), s32[]{:S(2)}) async-start(), calls=%async_computation | async-start | bytes 25165824 | tf_op jit(solution)/shard_map/psum | solution.py:181
  193.1 6.1 %copy-start.12 = (bf16[512,512]{0,1:T(8,128)(2,1)S(1)}, bf16[512,512]{0,1:T(8,128)(2,1)}, u32[]{:S(2)}) copy-start(bf16[512,512]{0,1:T(8,128)(2,1)} %copy-done.11) | copy-start | bytes 1572868
  193.1 6.1 %copy-start.28 = (bf16[512,8,64]{0,2,1:T(8,128)(2,1)S(1)}, bf16[512,8,64]{0,2,1:T(8,128)(2,1)}, u32[]{:S(2)}) copy-start(bf16[512,8,64]{0,2,1:T(8,128)(2,1)} %copy-done.27) | copy-start | bytes 1572868
  193.1 7.5 %copy-start.26 = (bf16[512,512]{0,1:T(8,128)(2,1)S(1)}, bf16[512,512]{0,1:T(8,128)(2,1)}, u32[]{:S(2)}) copy-start(bf16[512,512]{0,1:T(8,128)(2,1)} %copy-done.25) | copy-start | bytes 1572868
  199.1 2.0 copy-start.4
  200.6 2.0 copy-start.21
  202.7 3.4 copy-start.16
  202.7 3.4 copy-start.35
  305.9 5.5 %copy-start.22 = (bf16[512,8,256]{2,0,1:T(8,128)(2,1)S(1)}, bf16[512,8,256]{2,0,1:T(8,128)(2,1)}, u32[]{:S(2)}) copy-start(bf16[512,8,256]{2,0,1:T(8,128)(2,1)} %copy.24) | copy-start | bytes 6291460
  311.4 7.0 %copy-start.53 = (bf16[512,512]{0,1:T(8,128)(2,1)S(1)}, bf16[512,512]{0,1:T(8,128)(2,1)}, u32[]{:S(2)}) copy-start(bf16[512,512]{0,1:T(8,128)(2,1)} %copy-done.52) | copy-start | bytes 1572868
  318.4 9.4 %copy-start.41 = (bf16[8,64,512]{2,1,0:T(8,128)(2,1)}, bf16[8,64,512]{2,1,0:T(8,128)(2,1)S(1)}, u32[]{:S(2)}) copy-start(bf16[8,64,512]{2,1,0:T(8,128)(2,1)S(1)} %fusion.71) | copy-start | bytes 1572868
  318.4 2.4 copy-start.7
  318.5 2.4 copy-start.29
  318.5 2.4 copy-start.47
  320.8 3.2 copy-start.45
  329.4 5.9 %copy-start.38 = (bf16[512,512]{1,0:T(8,128)(2,1)S(1)}, bf16[512,512]{1,0:T(8,128)(2,1)}, u32[]{:S(2)}) copy-start(bf16[512,512]{1,0:T(8,128)(2,1)} %param.14) | copy-start | bytes 1572868
  335.2 2.2 copy-start.40
  335.2 2.2 copy-start.42
  335.7 2.9 copy-start.10
  335.7 2.9 copy-start.14
  501.0 4.8 copy-start.32
  501.0 5.8 %copy-start.31 = (f32[512,512]{1,0:T(8,128)S(1)}, f32[512,512]{1,0:T(8,128)}, u32[]{:S(2)}) copy-start(f32[512,512]{1,0:T(8,128)} %get-tuple-element.64) | copy-start | bytes 3145732
  501.0 6.7 %copy-start.18 = (f32[512,2048]{1,0:T(8,128)S(1)}, f32[512,2048]{1,0:T(8,128)}, u32[]{:S(2)}) copy-start(f32[512,2048]{1,0:T(8,128)} %get-tuple-element.65) | copy-start | bytes 12582916
  507.7 3.7 copy-start.17
  507.7 5.7 %copy-start.1 = (bf16[512,2048]{1,0:T(8,128)(2,1)S(1)}, bf16[512,2048]{1,0:T(8,128)(2,1)}, u32[]{:S(2)}) copy-start(bf16[512,2048]{1,0:T(8,128)(2,1)} %param.18) | copy-start | bytes 6291460
  (9 other events, 9.0 us)
Sparse Core Ops, SparseCore 0:
  30.7 117.1 all-reduce.11
  192.2 113.6 all-reduce.9
  329.5 171.4 all-reduce.7
where the time goes:
time: 528 us; the launch traced here: 520 us
  waiting for transfers between devices  300 us (57%)
  matrix products  89.4 us (17%)
  blocking collectives  65.7 us (12%)
  local copies, waits for them, and re-layouts  33.1 us (6%)
  other arithmetic  17 us (3%)
  between operations  14.8 us (3%)
    psum x1, waiting for transfers between devices, per_device(): summed_docs, summed_tots = lax.psum((local_summary, local_totals), 'seq')  111 us
    psum x1, waiting for transfers between devices, per_device(): lax.psum((local_grad_summary, local_grad_totals), 'seq')  96.1 us
    psum x1, waiting for transfers between devices, per_device(): lax.psum((grad_w_query, grad_w_key, grad_w_value, grad_w_output, grad_w_u...  93.1 us
    psum x1, blocking collectives, per_device(): lax.psum((grad_w_query, grad_w_key, grad_w_value, grad_w_output, grad_w_u...  65.7 us
    unnamed x118, local copies, waits for them, and re-layouts  25.1 us
    dot_general x12, matrix products, contract(): lax.dot_general(left_side, right_side, (((left_dim,), (right_dim,)), ((),...  20.9 us
  transfers between devices with their start and end apart: 3, of which 3 were waited for; matrix products, arithmetic and copies ran while one was open for 7% of the time, Pallas kernels for 0%

commit v1 on v0

--- a/solution.py
+++ b/solution.py
@@ -1,8 +1,11 @@
+import functools
 import math
 
 import jax
 import jax.numpy as jnp
 from jax import lax
+from jax.experimental import pallas as pl
+from jax.experimental.pallas import tpu as pltpu
 from jax.sharding import PartitionSpec as P
 
 SEGS = 10
@@ -34,8 +37,262 @@
     )
 
 
-def settle(local_part, arrived):
-    return local_part + (arrived - local_part)
+MESH = pl.DeviceIdType.MESH
+SLAB = 136
+COLORS = 6
+DIM_ORDER = (0, 2, 4, 1, 3, 5)
+
+
+def place():
+    pack, seq = lax.axis_index("pack"), lax.axis_index("seq")
+    return pack // 2, pack % 2, seq // 4, seq % 4
+
+
+def neighbour(dim, z, core, x, y):
+    axis = dim // 2
+    here = (x, y, z)[axis]
+    if dim % 2 == 0:
+        there, side = here + 1 - 2 * (here % 2), ((here + 1) // 2) % 2
+    else:
+        there, side = 3 - here, here // 2
+    x = there if axis == 0 else x
+    y = there if axis == 1 else y
+    z = there if axis == 2 else z
+    return (z * 2 + core, x * 4 + y), side
+
+
+def exchange(out_ref, in_ref, back_ref, got_ref, sems, pack, seq):
+    first = []
+    for step in range(1, 16):
+        peer = lax.rem(seq + step, 16)
+        copy = pltpu.make_async_remote_copy(
+            src_ref=out_ref.at[peer], dst_ref=in_ref.at[seq],
+            send_sem=sems.at[0, step - 1], recv_sem=sems.at[1, step - 1],
+            device_id=(pack, peer), device_id_type=MESH)
+        copy.start()
+        first.append(copy)
+    in_ref[seq] = out_ref[seq]
+    for copy in first:
+        copy.wait()
+    carry = jnp.zeros((64, 128), jnp.float32)
+    carry_tot = jnp.zeros((1, 128), jnp.float32)
+    for dev in range(16):
+        if dev > 0:
+            whole = in_ref[dev - 1, 130:131] == in_ref[dev - 1, 131:132]
+            joins = in_ref[dev - 1, 131:132] == in_ref[dev, 130:131]
+            carry = jnp.where(joins, in_ref[dev - 1, 64:128] + jnp.where(whole, carry, 0.0), 0.0)
+            carry_tot = jnp.where(joins, in_ref[dev - 1, 129:130] + jnp.where(whole, carry_tot, 0.0), 0.0)
+        back_ref[dev, 0:64] = carry
+        back_ref[dev, 128:129] = carry_tot
+    carry = jnp.zeros((64, 128), jnp.float32)
+    carry_tot = jnp.zeros((1, 128), jnp.float32)
+    for dev in reversed(range(16)):
+        if dev < 15:
+            whole = in_ref[dev + 1, 130:131] == in_ref[dev + 1, 131:132]
+            joins = in_ref[dev, 131:132] == in_ref[dev + 1, 130:131]
+            carry = jnp.where(joins, in_ref[dev + 1, 0:64] + jnp.where(whole, carry, 0.0), 0.0)
+            carry_tot = jnp.where(joins, in_ref[dev + 1, 128:129] + jnp.where(whole, carry_tot, 0.0), 0.0)
+        back_ref[dev, 64:128] = carry
+        back_ref[dev, 129:130] = carry_tot
+        back_ref[dev, 130:136] = jnp.zeros((6, 128), jnp.float32)
+    second = []
+    for step in range(1, 16):
+        peer = lax.rem(seq + step, 16)
+        copy = pltpu.make_async_remote_copy(
+            src_ref=back_ref.at[peer], dst_ref=got_ref.at[seq],
+            send_sem=sems.at[2, step - 1], recv_sem=sems.at[3, step - 1],
+            device_id=(pack, peer), device_id_type=MESH)
+        copy.start()
+        second.append(copy)
+    got_ref[seq] = back_ref[seq]
+    for copy in second:
+        copy.wait()
+
+
+def exchange_kernel(out_ref, got_ref, in_ref, back_ref, sems):
+    pack, seq = lax.axis_index("pack"), lax.axis_index("seq")
+    barrier = pltpu.get_barrier_semaphore()
+    for step in range(1, 16):
+        pl.semaphore_signal(barrier, inc=1, device_id=(pack, lax.rem(seq + step, 16)), device_id_type=MESH)
+    pl.semaphore_wait(barrier, 15)
+    exchange(out_ref, in_ref, back_ref, got_ref, sems, pack, seq)
+
+
+def document_ends(local_summary, local_totals, doc_rows):
+    first, last = doc_rows[0], doc_rows[-1]
+
+    def side(doc):
+        return (lax.dynamic_index_in_dim(local_summary, doc, 0, False),
+                lax.dynamic_index_in_dim(local_totals, doc, 0, False))
+
+    (sum_f, tot_f), (sum_l, tot_l) = side(first), side(last)
+    heads, feats, size = sum_f.shape
+    ids = jnp.broadcast_to(jnp.stack([first, last]).astype(jnp.float32)[None, :, None], (heads, 2, feats))
+    slab = jnp.concatenate(
+        [jnp.swapaxes(sum_f, 1, 2), jnp.swapaxes(sum_l, 1, 2), tot_f[:, None], tot_l[:, None], ids,
+         jnp.zeros((heads, 4, feats), jnp.float32)], axis=1)
+    slab = slab.reshape(heads, SLAB, 2, 128).swapaxes(1, 2).reshape(heads * 2, SLAB, 128)
+    vmem = pltpu.VMEM((16, SLAB, 128), jnp.float32)
+    got = pl.pallas_call(
+        exchange_kernel,
+        out_shape=jax.ShapeDtypeStruct((16, SLAB, 128), jnp.float32),
+        in_specs=[pl.BlockSpec(memory_space=pltpu.VMEM)],
+        out_specs=pl.BlockSpec(memory_space=pltpu.VMEM),
+        scratch_shapes=[vmem, vmem, pltpu.SemaphoreType.DMA((4, 15))],
+        compiler_params=pltpu.CompilerParams(collective_id=0, has_side_effects=True, vmem_limit_bytes=32 * 2**20),
+    )(slab)
+    got = got.reshape(heads, 2, SLAB, 128).swapaxes(1, 2).reshape(heads, SLAB, 256)
+    docs = jnp.arange(SEGS, dtype=jnp.int32)
+    at_f = (docs == first).astype(jnp.float32)
+    at_l = (docs == last).astype(jnp.float32)
+    sum_a, sum_b = jnp.swapaxes(got[:, 0:64], 1, 2), jnp.swapaxes(got[:, 64:128], 1, 2)
+    tot_a, tot_b = got[:, 128], got[:, 129]
+    w = lambda at, v: at.reshape((SEGS,) + (1,) * v.ndim) * v[None]
+    return (local_summary + w(at_f, sum_a) + w(at_l, sum_b), local_totals + w(at_f, tot_a) + w(at_l, tot_b))
+
+
+def add_rows(dst, dst_row, src, src_row, count):
+    step = min(64, count)
+
+    def body(i, _):
+        dst[pl.ds(pl.multiple_of(dst_row + i * step, 8), step), :] += src[pl.ds(pl.multiple_of(src_row + i * step, 8), step), :]
+        return 0
+
+    lax.fori_loop(0, count // step, body, 0)
+
+
+def weights_kernel(rows, g_hbm, gain_ref, o_hbm, gain_out, g, from_core, from_chip, gain_buf, gain_mid, gain_all, turn, ssem, rsem, gsem, free, lsem):
+    z, core, x, y = place()
+    pack, seq = lax.axis_index("pack"), lax.axis_index("seq")
+    load = pltpu.make_async_copy(g_hbm, g, lsem)
+    load.start()
+    barrier = pltpu.get_barrier_semaphore()
+    sibling = (z * 2 + 1 - core, seq)
+    for step in range(1, 16):
+        pl.semaphore_signal(barrier, inc=1, device_id=(pack, lax.rem(seq + step, 16)), device_id_type=MESH)
+    for step in range(1, 8):
+        pl.semaphore_signal(barrier, inc=1, device_id=(lax.rem(pack + step, 8), seq), device_id_type=MESH)
+    pl.semaphore_wait(barrier, 22)
+    gain_copies = []
+    for step in range(1, 8):
+        copy = pltpu.make_async_remote_copy(
+            src_ref=gain_ref, dst_ref=gain_buf.at[step - 1], send_sem=gsem.at[0, step - 1], recv_sem=gsem.at[1, step - 1],
+            device_id=(lax.rem(pack + step, 8), seq), device_id_type=MESH)
+        copy.start()
+        gain_copies.append(copy)
+    load.wait()
+    n = rows // 2 // COLORS
+    copies = []
+    for k in range(COLORS):
+        copy = pltpu.make_async_remote_copy(
+            src_ref=g.at[pl.ds(pl.multiple_of(k * 2 * n + (1 - core) * n, 8), n)], dst_ref=from_core.at[k],
+            send_sem=ssem.at[k, 0], recv_sem=rsem.at[k, 0], device_id=sibling, device_id_type=MESH)
+        copy.start()
+        copies.append(copy)
+    for copy in gain_copies:
+        copy.wait()
+    total = gain_ref[...]
+    for step in range(7):
+        total = total + gain_buf[step]
+    gain_mid[...] = total
+    gain_copies = []
+    for step in range(1, 16):
+        copy = pltpu.make_async_remote_copy(
+            src_ref=gain_mid, dst_ref=gain_all.at[step - 1], send_sem=gsem.at[2, step - 1], recv_sem=gsem.at[3, step - 1],
+            device_id=(pack, lax.rem(seq + step, 16)), device_id_type=MESH)
+        copy.start()
+        gain_copies.append(copy)
+    offs = []
+    for k in range(COLORS):
+        copies[k].wait()
+        pl.semaphore_signal(free.at[k, 6], inc=1, device_id=sibling, device_id_type=MESH)
+        add_rows(g, k * 2 * n + core * n, from_core.at[k], 0, n)
+        offs.append(k * 2 * n + core * n)
+    for s in range(6):
+        h = n >> (s + 1)
+        for k in range(COLORS):
+            dev, side = neighbour(DIM_ORDER[(k + s) % 6], z, core, x, y)
+            copies[k] = pltpu.make_async_remote_copy(
+                src_ref=g.at[pl.ds(pl.multiple_of(offs[k] + (1 - side) * h, 8), h)], dst_ref=from_chip.at[k, pl.ds(n - 2 * h, h)],
+                send_sem=ssem.at[k, s + 1], recv_sem=rsem.at[k, s + 1], device_id=dev, device_id_type=MESH)
+            copies[k].start()
+        for k in range(COLORS):
+            dev, side = neighbour(DIM_ORDER[(k + s) % 6], z, core, x, y)
+            offs[k] = offs[k] + side * h
+            copies[k].wait()
+            if s < 5:
+                pl.semaphore_signal(free.at[k, s], inc=1, device_id=dev, device_id_type=MESH)
+            add_rows(g, offs[k], from_chip.at[k], n - 2 * h, h)
+    for s in reversed(range(6)):
+        h = n >> (s + 1)
+        for k in range(COLORS):
+            dev, side = neighbour(DIM_ORDER[(k + s) % 6], z, core, x, y)
+            part = g.at[pl.ds(pl.multiple_of(offs[k], 8), h)]
+            if s < 5:
+                pl.semaphore_wait(free.at[k, s], 1)
+            copies[k] = pltpu.make_async_remote_copy(
+                src_ref=part, dst_ref=part if s < 5 else turn.at[k], send_sem=ssem.at[k, 7 + s], recv_sem=rsem.at[k, 7 + s], device_id=dev, device_id_type=MESH)
+            copies[k].start()
+        for k in range(COLORS):
+            dev, side = neighbour(DIM_ORDER[(k + s) % 6], z, core, x, y)
+            copies[k].wait()
+            if s == 5:
+                g[pl.ds(pl.multiple_of(offs[k] + (1 - 2 * side) * h, 8), h)] = turn[k]
+            offs[k] = offs[k] - side * h
+    for k in range(COLORS):
+        part = g.at[pl.ds(pl.multiple_of(offs[k], 8), n)]
+        pl.semaphore_wait(free.at[k, 6], 1)
+        copies[k] = pltpu.make_async_remote_copy(
+            src_ref=part, dst_ref=part, send_sem=ssem.at[k, 13], recv_sem=rsem.at[k, 13], device_id=sibling, device_id_type=MESH)
+        copies[k].start()
+    for copy in gain_copies:
+        copy.wait()
+    total = gain_mid[...]
+    for step in range(15):
+        total = total + gain_all[step]
+    gain_out[...] = total
+    stores = []
+    for k in range(COLORS):
+        copies[k].wait()
+        part = pl.ds(k * 2 * n, 2 * n)
+        store = pltpu.make_async_copy(g.at[part], o_hbm.at[part], ssem.at[k, 14])
+        store.start()
+        stores.append(store)
+    for store in stores:
+        store.wait()
+
+
+def sum_weights(grad_w, gains):
+    wq, wk, wv, wo, up, down = grad_w
+    whole = jnp.concatenate([wq, wk, wv, wo] + [up[:, i * 512:(i + 1) * 512] for i in range(4)] + [down], axis=0)
+    rows = whole.shape[0]
+    n = rows // 2 // COLORS
+    gain = jnp.concatenate(gains).reshape(8, 128)
+    whole, gain = pl.pallas_call(
+        functools.partial(weights_kernel, rows),
+        out_shape=(jax.ShapeDtypeStruct((rows, 512), jnp.float32), jax.ShapeDtypeStruct((8, 128), jnp.float32)),
+        in_specs=[pl.BlockSpec(memory_space=pl.ANY), pl.BlockSpec(memory_space=pltpu.VMEM)],
+        out_specs=(pl.BlockSpec(memory_space=pl.ANY), pl.BlockSpec(memory_space=pltpu.VMEM)),
+        scratch_shapes=[
+            pltpu.VMEM((rows, 512), jnp.float32),
+            pltpu.VMEM((COLORS, n, 512), jnp.float32),
+            pltpu.VMEM((COLORS, n, 512), jnp.float32),
+            pltpu.VMEM((7, 8, 128), jnp.float32),
+            pltpu.VMEM((8, 128), jnp.float32),
+            pltpu.VMEM((15, 8, 128), jnp.float32),
+            pltpu.VMEM((COLORS, 8, 512), jnp.float32),
+            pltpu.SemaphoreType.DMA((COLORS, 15)),
+            pltpu.SemaphoreType.DMA((COLORS, 15)),
+            pltpu.SemaphoreType.DMA((4, 15)),
+            pltpu.SemaphoreType.REGULAR((COLORS, 7)),
+            pltpu.SemaphoreType.DMA,
+        ],
+        compiler_params=pltpu.CompilerParams(collective_id=1, has_side_effects=True, vmem_limit_bytes=60 * 2**20),
+    )(whole, gain)
+    block = lambda i: whole[i * 512:(i + 1) * 512]
+    flat = gain.reshape(1024)
+    return (block(0), block(1), block(2), block(3), jnp.concatenate([block(4 + i) for i in range(4)], axis=1),
+            whole[4096:6144], flat[:512], flat[512:])
 
 
 def per_device(
@@ -85,9 +342,7 @@
         "tshm,thd->shmd", masked_key, value_head_rows, preferred_element_type=jnp.float32
     )
     local_totals = jnp.einsum("ts,thm->shm", onehot, phi_key, preferred_element_type=jnp.float32)
-    summed_docs, summed_tots = lax.psum((local_summary, local_totals), "seq")
-    summary = settle(local_summary, summed_docs)
-    totals = settle(local_totals, summed_tots)
+    summary, totals = document_ends(local_summary, local_totals, doc_rows)
     summary_low = summary.astype(jnp.bfloat16)
     masked_query = phi_query[:, None, :, :] * onehot_mask
     numerator = jnp.einsum(
@@ -136,9 +391,7 @@
         phi_query.astype(jnp.float32) * grad_denominator[:, :, None],
         precision=highest_precision_flag,
     )
-    summed_grad_docs, summed_grad_tots = lax.psum((local_grad_summary, local_grad_totals), "seq")
-    grad_summary = settle(local_grad_summary, summed_grad_docs)
-    grad_totals = settle(local_grad_totals, summed_grad_tots)
+    grad_summary, grad_totals = document_ends(local_grad_summary, local_grad_totals, doc_rows)
     grad_summary_low = grad_summary.astype(jnp.bfloat16)
     masked_value = value_head_rows[:, None, :, :] * onehot_mask
     grad_phi_key = jnp.einsum(
@@ -178,18 +431,8 @@
     grad_w_value = contract(normed, grad_value, 0, 0)
     grad_rows_norm, grad_gain_attn = norm_pull_attn(grad_normed.astype(jnp.float32))
     grad_inputs = grad_middle + grad_rows_norm
-    summed = lax.psum(
-        (
-            grad_w_query,
-            grad_w_key,
-            grad_w_value,
-            grad_w_output,
-            grad_w_up,
-            grad_w_down,
-            grad_gain_attn,
-            grad_gain_ffn,
-        ),
-        ("pack", "seq"),
+    summed = sum_weights(
+        (grad_w_query, grad_w_key, grad_w_value, grad_w_output, grad_w_up, grad_w_down), (grad_gain_attn, grad_gain_ffn)
     )
     return (
         outputs[None].astype(jnp.bfloat16),

time: 528 us -> 350 us (0.66)
  waiting for transfers between devices: 300 us -> 0 us
  Pallas kernels: 0 us -> 180 us
  blocking collectives: 65.7 us -> 0 us
  local copies, waits for them, and re-layouts: 33.1 us -> 56.4 us
  between operations: 14.8 us -> 5.71 us
    psum x3 -> x0, waiting for transfers between devices: 300 us -> none  [the longest x1 111 us: per_device(): summed_docs, summed_tots = lax.psum((local_summary, local_totals), 'seq')]
    pallas_call x0 -> x3, Pallas kernels: none -> 180 us  [the longest x1 109 us: sum_weights(): pl.pallas_call(functools.partial(weights_kernel, rows), out_shape=(jax.Sh...]
    psum x1 -> x0, blocking collectives: 65.7 us -> none  [per_device(): lax.psum((grad_w_query, grad_w_key, grad_w_value, grad_w_output, grad_w_u...]
    slice x0 -> x6, local copies, waits for them, and re-layouts: none -> 13.7 us  [the longest x1 6.06 us: sum_weights(): block = lambda i: whole[i * 512:(i + 1) * 512]]
    unnamed x118 -> x175, local copies, waits for them, and re-layouts: 25.1 us -> 20 us
  transfers between devices with their start and end apart: 3 -> 0, of which waited for: 3 -> 0; matrix products, arithmetic and copies ran while one was open for 7% -> 0% of each run, Pallas kernels for 0% -> 0%
where the time goes in v1:
time: 350 us; the launch traced here: 346 us
  Pallas kernels  180 us (51%)
  matrix products  87 us (25%)
  local copies, waits for them, and re-layouts  56.4 us (16%)
  other arithmetic  16.1 us (5%)
  between operations  5.71 us (2%)
    pallas_call x1, Pallas kernels, sum_weights(): pl.pallas_call(functools.partial(weights_kernel, rows), out_shape=(jax.Sh...  109 us
    pallas_call x2, Pallas kernels, document_ends(): pl.pallas_call(exchange_kernel, out_shape=jax.ShapeDtypeStruct((16, SLAB,...  71.4 us
    dot_general x12, matrix products, contract(): lax.dot_general(left_side, right_side, (((left_dim,), (right_dim,)), ((),...  23.7 us
    unnamed x175, local copies, waits for them, and re-layouts  20 us
    dot_general x1, matrix products, per_device(): jnp.einsum('tshm,shmd->thd', masked_query, summary_low, preferred_element...  9.8 us
    dot_general x1, matrix products, per_device(): jnp.einsum('ts,shm->thm', onehot_float, totals, precision=highest_precisi...  7.9 us
    dot_general x1, matrix products, per_device(): jnp.einsum('tshm,thd->shmd', masked_key, value_head_rows, preferred_eleme...  7.48 us

profile of v1, /device:TPU:1, one launch (start us, length us, event | category | flops | bytes accessed | tf_op | source)
XLA Modules:
  0.0 345.5 jit_solution(3285831087642291095)
XLA Ops:
  0.7 1.4 copy.36
  2.5 1.6 fusion.83
  4.1 2.8 fusion.151
  7.6 3.0 multiply_convert_fusion.4
  11.3 1.3 convolution_convert_fusion.5
  12.7 4.1 %copy.37 = bf16[512,8,256]{2,0,1:T(8,128)(2,1)} copy(bf16[512,8,256]{0,2,1:T(8,128)(2,1)} %copy-done.6) | data formatting | bytes 4194304 | tf_op jit(solution)/shard_map/convert_element_type | solution.py:339
  16.8 7.5 %fusion.6 = f32[8,64,10,256]{3,1,2,0:T(8,128)} fusion(bf16[512,8,64,1]{0,2,3,1:T(8,128)(2,1)S(1)} %bitcast.317, bf16[512,10]{0,1:T(8,128)(2,1)S(1)} %fusion.119, bf16[512,8,256]{2,0,1:T(8,128)(2,1)} %copy.37), kind=kOutput, calls=%fused_computation.6 | convolution fusion | flops 1384120320 | bytes 7874560 | tf_op jit(solution)/shard_map/tshm,thd->shmd/dot_general | solution.py:341
  28.4 2.3 dynamic-slice_bitcast_fusion.2
  32.7 2.9 concatenate.30
  35.7 36.5 %shard_map.204 = f32[16,136,128]{2,1,0:T(8,128)S(1)} custom-call(f32[16,136,128]{2,1,0:T(8,128)S(1)} %bitcast.284), custom_call_target="tpu_custom_call" | custom-call | tf_op jit(solution)/shard_map/pallas_call | solution.py:136
  72.8 1.9 reshape.322
  76.9 7.9 %fusion.24 = (f32[512,8]{0,1:T(8,128)S(1)}, bf16[512,8,256]{0,2,1:T(8,128)(2,1)}, f32[512,8,256]{0,2,1:T(8,128)}) fusion(f32[512,8]{0,1:T(8,128)S(1)} %broadcast_multiply_fusion, f32[8,512,256]{1,2,0:T(8,128)} %fusion.151, f32[10,8,256]{2,0,1:T(8,128)} %copy-done.35, f32[8,256]{1,0:T(8,128)S(1)} %get-tuple-element.93, f32[10]{0:T(128)S(1)} %get-tuple-element.95, ...), kind=kOutput, calls=%fused_computation.32 | convolution fusion | flops 133252096 | bytes 10618960 | tf_op jit(solution)/shard_map/ts,shm->thm/dot_general | solution.py:351
  85.0 2.6 fusion.19
  87.6 3.9 %copy.41 = bf16[512,8,256]{2,0,1:T(8,128)(2,1)} copy(bf16[512,8,256]{0,2,1:T(8,128)(2,1)} %get-tuple-element.39) | data formatting | bytes 4194304 | tf_op jit(solution)/shard_map/convert_element_type | solution.py:338
  91.5 9.8 %divide_convert_fusion = (bf16[512,8,64]{0,2,1:T(8,128)(2,1)S(1)}, f32[512,8,64]{0,2,1:T(8,128)}) fusion(f32[512,8]{0,1:T(8,128)S(1)} %get-tuple-element.38, bf16[10,8,256,64]{2,3,0,1:T(8,128)(2,1)} %fusion.19, bf16[512,8,256]{2,0,1:T(8,128)(2,1)} %copy.41, bf16[512,10]{0,1:T(8,128)(2,1)S(1)} %copy-done.67), kind=kOutput, calls=%fused_computation.148 | convolution fusion | flops 1353187328 | bytes 6318080 | tf_op jit(solution)/shard_map/tshm,shmd->thd/dot_general | solution.py:348
  102.1 1.4 fusion.135
  103.5 1.9 copy-done.18
  105.5 2.7 fusion.77
  108.2 2.0 copy.49
  110.2 2.0 copy.43
  112.3 6.2 %fusion.28 = bf16[512,2048]{1,0:T(8,128)(2,1)S(1)} fusion(f32[512,2048]{1,0:T(8,128)} %copy-done.18, bf16[2048,512]{1,0:T(8,128)(2,1)} %param.19, bf16[1,512,512]{2,1,0:T(8,128)(2,1)} %param.25), kind=kOutput, calls=%fused_computation.36 | convolution fusion | flops 1096810496 | bytes 8912896 | tf_op jit(solution)/shard_map/dot_general | solution.py:32
  118.5 1.3 fusion.80
  122.4 1.4 copy-done.8
  124.5 3.0 fusion.150
  128.6 1.4 fusion.152
  130.0 2.2 fusion.25
  132.2 4.3 %fusion = f32[8,64,10,256]{3,1,2,0:T(8,128)S(1)} fusion(bf16[512,8,256]{2,0,1:T(8,128)(2,1)S(1)} %copy-done.26, bf16[512,10]{0,1:T(8,128)(2,1)S(1)} %copy-done.68, bf16[512,8,64]{0,2,1:T(8,128)(2,1)S(1)} %fusion.87), kind=kOutput, calls=%fused_computation | convolution fusion | flops 1384120320 | bytes 7874560 | tf_op jit(solution)/shard_map/tshm,thd->shmd/dot_general | solution.py:385
  136.5 2.3 copy-done.9
  139.7 1.4 concatenate.32
  141.3 34.8 %shard_map.205 = f32[16,136,128]{2,1,0:T(8,128)S(1)} custom-call(f32[16,136,128]{2,1,0:T(8,128)S(1)} %bitcast.285), custom_call_target="tpu_custom_call" | custom-call | tf_op jit(solution)/shard_map/pallas_call | solution.py:136
  176.8 1.9 reshape.329
  180.9 3.5 %fusion.17 = bf16[10,8,256,64]{2,3,0,1:T(8,128)(2,1)S(1)} fusion(f32[8,64,10,256]{3,1,2,0:T(8,128)} %copy-done.9, f32[8,256,64]{1,2,0:T(8,128)S(1)} %get-tuple-element.55, f32[8,256,64]{1,2,0:T(8,128)S(1)} %get-tuple-element.54, f32[10]{0:T(128)S(1)} %copy-done.71, f32[10]{0:T(128)S(1)} %copy-done.73), kind=kLoop, calls=%fused_computation.24 | loop fusion | flops 6553600 | bytes 8912976 | tf_op jit(solution)/shard_map/convert_element_type | solution.py:395
  184.5 1.8 fusion.20
  186.7 3.3 fusion.49
  190.0 1.5 fusion.72
  192.1 6.9 %fusion.67 = bf16[8,64,512]{2,1,0:T(8,128)(2,1)S(1)} fusion(bf16[10,8,256,64]{2,3,0,1:T(8,128)(2,1)S(1)} %fusion.17, bf16[512,10]{0,1:T(8,128)(2,1)S(1)} %copy-done.69, bf16[512,8,256]{2,0,1:T(8,128)(2,1)S(1)} %copy-done.25), kind=kOutput, calls=%fused_computation.106 | convolution fusion | flops 1352925184 | bytes 5253120 | tf_op jit(solution)/shard_map/tshm,shmd->thd/dot_general | solution.py:404
  200.5 1.5 fusion.100
  202.1 2.2 copy.50
  204.2 2.7 convolution_dynamic-update-slice_fusion.4
  206.9 2.5 convolution_dynamic-update-slice_fusion.3
  209.5 1.5 convolution_dynamic-update-slice_fusion.2
  210.9 1.4 convolution_dynamic-update-slice_fusion.1
  212.4 1.3 fusion.134
  218.2 3.9 %convolution_dynamic-update-slice_fusion.g_hbm = f32[6144,512]{1,0:T(8,128)} fusion(f32[6144,512]{1,0:T(8,128)} %slice_dynamic-update-slice_fusion, bf16[1,512,512]{2,1,0:T(8,128)(2,1)S(1)} %copy-done.38, f32[512,2048]{1,0:T(8,128)S(1)} %copy-done.19), kind=kOutput, calls=%fused_computation.60 | convolution fusion | flops 1083179008 | bytes 8912896 | tf_op jit(solution)/shard_map/dot_general | solution.py:32
  222.7 108.9 %shard_map.206 = (f32[6144,512]{1,0:T(8,128)}, f32[8,128]{1,0:T(8,128)}) custom-call(f32[6144,512]{1,0:T(8,128)} %convolution_dynamic-update-slice_fusion.g_hbm, f32[8,128]{1,0:T(8,128)} %pad_maximum_fusion.3.gain_ref), custom_call_target="tpu_custom_call" | custom-call | tf_op jit(solution)/shard_map/pallas_call | solution.py:271
  331.6 6.1 %fusion.143 = (f32[512,512]{1,0:T(8,128)S(1)}, f32[512,512]{1,0:T(8,128)S(1)}, f32[512,512]{1,0:T(8,128)S(1)}, f32[512,512]{1,0:T(8,128)S(1)}, f32[512,512]{1,0:...) fusion(f32[6144,512]{1,0:T(8,128)} %get-tuple-element.12), kind=kLoop, calls=%fused_computation.225 | loop fusion | bytes 16777216 | tf_op jit(solution)/shard_map/slice | solution.py:292
  337.6 2.4 pad_maximum_fusion
  340.0 4.6 %slice.123 = f32[2048,512]{1,0:T(8,128)} slice(f32[6144,512]{1,0:T(8,128)} %get-tuple-element.12), slice={[4096:6144], [0:512]} | slice | bytes 8388608 | tf_op jit(solution)/shard_map/slice | solution.py:295
  (219 shorter events, 23.7 us)
Async XLA Ops:
  0.6 101.5 %copy-start = (bf16[512,2048]{1,0:T(8,128)(2,1)S(1)}, bf16[512,2048]{1,0:T(8,128)(2,1)}, u32[]{:S(2)}) copy-start(bf16[512,2048]{1,0:T(8,128)(2,1)} %param.18) | copy-start | bytes 6291460
  2.1 9.2 %copy-start.2 = (bf16[1,512,512]{1,2,0:T(8,128)(2,1)}, bf16[1,512,512]{1,2,0:T(8,128)(2,1)S(1)}, u32[]{:S(2)}) copy-start(bf16[1,512,512]{1,2,0:T(8,128)(2,1)S(1)} %copy.36) | copy-start | bytes 1572868
  2.2 4.7 %copy-start.76 = (s32[1,512]{1,0:T(1,128)S(1)}, s32[1,512]{1,0:T(1,128)}, u32[]{:S(2)}) copy-start(s32[1,512]{1,0:T(1,128)} %param.24) | copy-start | bytes 6148
  2.2 4.7 %copy-start.40 = (bf16[512,512]{1,0:T(8,128)(2,1)S(1)}, bf16[512,512]{1,0:T(8,128)(2,1)}, u32[]{:S(2)}) copy-start(bf16[512,512]{1,0:T(8,128)(2,1)} %param.15) | copy-start | bytes 1572868
  2.2 4.7 %copy-start.62 = (f32[512]{0:T(512)S(1)}, f32[512]{0:T(512)}, u32[]{:S(2)}) copy-start(f32[512]{0:T(512)} %param.20) | copy-start | bytes 6148
  2.3 9.0 %copy-start.52 = (f32[512]{0:T(512)}, f32[512]{0:T(512)S(1)}, u32[]{:S(2)}) copy-start(f32[512]{0:T(512)S(1)} %broadcast_multiply_fusion.4) | copy-start | bytes 6148
  2.4 5.1 %copy-start.58 = (f32[512]{0:T(512)}, f32[512]{0:T(512)S(1)}, u32[]{:S(2)}) copy-start(f32[512]{0:T(512)S(1)} %fusion.89) | copy-start | bytes 6148
  2.5 8.8 %copy-start.56 = (f32[512]{0:T(512)}, f32[512]{0:T(512)S(1)}, u32[]{:S(2)}) copy-start(f32[512]{0:T(512)S(1)} %fusion.129) | copy-start | bytes 6148
  4.1 6.5 %copy-start.31 = (bf16[512,512]{0,1:T(8,128)(2,1)}, bf16[512,512]{0,1:T(8,128)(2,1)S(1)}, u32[]{:S(2)}) copy-start(bf16[512,512]{0,1:T(8,128)(2,1)S(1)} %get-tuple-element.77) | copy-start | bytes 1572868
  7.5 3.8 %copy-start.47 = (bf16[512,512]{0,1:T(8,128)(2,1)}, bf16[512,512]{0,1:T(8,128)(2,1)S(1)}, u32[]{:S(2)}) copy-start(bf16[512,512]{0,1:T(8,128)(2,1)S(1)} %get-tuple-element.73) | copy-start | bytes 1572868
  7.5 3.7 %copy-start.42 = (bf16[512,512]{1,0:T(8,128)(2,1)S(1)}, bf16[512,512]{1,0:T(8,128)(2,1)}, u32[]{:S(2)}) copy-start(bf16[512,512]{1,0:T(8,128)(2,1)} %param.16) | copy-start | bytes 1572868
  11.3 19.4 %copy-start.35 = (f32[10,8,256]{2,0,1:T(8,128)}, f32[10,8,256]{2,0,1:T(8,128)S(1)}, u32[]{:S(2)}) copy-start(f32[10,8,256]{2,0,1:T(8,128)S(1)} %fusion.123) | copy-start | bytes 245764
  12.6 4.1 %copy-start.78 = (bf16[512,512]{0,1:T(8,128)(2,1)S(1)}, bf16[512,512]{0,1:T(8,128)(2,1)}, u32[]{:S(2)}) copy-start(bf16[512,512]{0,1:T(8,128)(2,1)} %convolution_convert_fusion.5) | copy-start | bytes 1572868
  12.7 11.6 %copy-start.66 = (bf16[512,10]{0,1:T(8,128)(2,1)}, bf16[512,10]{0,1:T(8,128)(2,1)S(1)}, u32[]{:S(2)}) copy-start(bf16[512,10]{0,1:T(8,128)(2,1)S(1)} %fusion.119) | copy-start | bytes 30724
  76.9 8.1 %copy-start.70 = (f32[10]{0:T(128)}, f32[10]{0:T(128)S(1)}, u32[]{:S(2)}) copy-start(f32[10]{0:T(128)S(1)} %get-tuple-element.95) | copy-start | bytes 124
  76.9 8.1 %copy-start.72 = (f32[10]{0:T(128)}, f32[10]{0:T(128)S(1)}, u32[]{:S(2)}) copy-start(f32[10]{0:T(128)S(1)} %get-tuple-element.96) | copy-start | bytes 124
  76.9 8.1 %slice-start = ((s8[5242880]{0:T(1024)(128)(4,1)}), s8[4194304]{0:T(1024)(128)(4,1)S(1)}, s32[]{:S(2)}) async-start(s8[5242880]{0:T(1024)(128)(4,1)} %bitcast.288), calls=%async_computation | async-start | bytes 8388608
  76.9 7.9 %copy-start.16 = (f32[8,136,256]{2,1,0:T(8,128)S(1)}, f32[8,136,256]{2,1,0:T(8,128)}, u32[]{:S(2)}) copy-start(f32[8,136,256]{2,1,0:T(8,128)} %reshape.322) | copy-start | bytes 3342340
  76.9 8.1 %slice-start.1 = ((s8[5242880]{0:T(1024)(128)(4,1)}), s8[1048576]{0:T(1024)(128)(4,1)S(1)}, s32[]{:S(2)}) async-start(s8[5242880]{0:T(1024)(128)(4,1)} %bitcast.288), calls=%async_computation.1 | async-start | bytes 2097152
  87.6 3.9 %copy-start.67 = (bf16[512,10]{0,1:T(8,128)(2,1)S(1)}, bf16[512,10]{0,1:T(8,128)(2,1)}, u32[]{:S(2)}) copy-start(bf16[512,10]{0,1:T(8,128)(2,1)} %copy-done.66) | copy-start | bytes 30724
  91.5 9.8 %copy-start.3 = (bf16[1,512,512]{1,2,0:T(8,128)(2,1)S(1)}, bf16[1,512,512]{1,2,0:T(8,128)(2,1)}, u32[]{:S(2)}) copy-start(bf16[1,512,512]{1,2,0:T(8,128)(2,1)} %copy-done.2) | copy-start | bytes 1572868
  91.5 9.9 %copy-start.27 = (bf16[512,512]{1,0:T(8,128)(2,1)S(1)}, bf16[512,512]{1,0:T(8,128)(2,1)}, u32[]{:S(2)}) copy-start(bf16[512,512]{1,0:T(8,128)(2,1)} %param.17) | copy-start | bytes 1572868
  91.5 10.6 %copy-start.49 = (f32[512]{0:T(512)S(1)}, f32[512]{0:T(512)}, u32[]{:S(2)}) copy-start(f32[512]{0:T(512)} %param.21) | copy-start | bytes 6148
  118.5 3.8 %copy-start.20 = (f32[512,8,256]{0,2,1:T(8,128)S(1)}, f32[512,8,256]{0,2,1:T(8,128)}, u32[]{:S(2)}) copy-start(f32[512,8,256]{0,2,1:T(8,128)} %get-tuple-element.78) | copy-start | bytes 12582916
  119.9 3.9 %copy-start.8 = (f32[8,512,256]{1,2,0:T(8,128)S(1)}, f32[8,512,256]{1,2,0:T(8,128)}, u32[]{:S(2)}) copy-start(f32[8,512,256]{1,2,0:T(8,128)} %fusion.151) | copy-start | bytes 12582916
  119.9 4.7 %copy-start.21 = (bf16[10,8,256,64]{2,3,0,1:T(8,128)(2,1)S(1)}, bf16[10,8,256,64]{2,3,0,1:T(8,128)(2,1)}, u32[]{:S(2)}) copy-start(bf16[10,8,256,64]{2,3,0,1:T(8,128)(2,1)} %fusion.19) | copy-start | bytes 7864324
  119.9 4.6 %copy-start.68 = (bf16[512,10]{0,1:T(8,128)(2,1)S(1)}, bf16[512,10]{0,1:T(8,128)(2,1)}, u32[]{:S(2)}) copy-start(bf16[512,10]{0,1:T(8,128)(2,1)} %copy-done.66) | copy-start | bytes 30724
  127.6 4.6 %copy-start.26 = (bf16[512,8,256]{2,0,1:T(8,128)(2,1)S(1)}, bf16[512,8,256]{2,0,1:T(8,128)(2,1)}, u32[]{:S(2)}) copy-start(bf16[512,8,256]{2,0,1:T(8,128)(2,1)} %copy.41) | copy-start | bytes 6291460
  128.1 8.4 %copy-start.33 = (bf16[512,8,64]{0,2,1:T(8,128)(2,1)}, bf16[512,8,64]{0,2,1:T(8,128)(2,1)S(1)}, u32[]{:S(2)}) copy-start(bf16[512,8,64]{0,2,1:T(8,128)(2,1)S(1)} %fusion.70) | copy-start | bytes 1572868
  132.2 7.5 %copy-start.36 = (f32[10,8,256]{2,0,1:T(8,128)}, f32[10,8,256]{2,0,1:T(8,128)S(1)}, u32[]{:S(2)}) copy-start(f32[10,8,256]{2,0,1:T(8,128)S(1)} %fusion.25) | copy-start | bytes 245764
  141.3 39.6 %copy-start.71 = (f32[10]{0:T(128)S(1)}, f32[10]{0:T(128)}, u32[]{:S(2)}) copy-start(f32[10]{0:T(128)} %copy-done.70) | copy-start | bytes 124
  141.3 39.6 %copy-start.73 = (f32[10]{0:T(128)S(1)}, f32[10]{0:T(128)}, u32[]{:S(2)}) copy-start(f32[10]{0:T(128)} %copy-done.72) | copy-start | bytes 124
  191.6 7.5 %copy-start.44 = (bf16[512,8,64]{0,2,1:T(8,128)(2,1)}, bf16[512,8,64]{0,2,1:T(8,128)(2,1)S(1)}, u32[]{:S(2)}) copy-start(bf16[512,8,64]{0,2,1:T(8,128)(2,1)S(1)} %fusion.72) | copy-start | bytes 1572868
  192.1 7.0 %copy-start.4 = (bf16[1,512,512]{1,2,0:T(8,128)(2,1)S(1)}, bf16[1,512,512]{1,2,0:T(8,128)(2,1)}, u32[]{:S(2)}) copy-start(bf16[1,512,512]{1,2,0:T(8,128)(2,1)} %copy-done.2) | copy-start | bytes 1572868
  192.1 7.1 %copy-start.43 = (bf16[512,512]{1,0:T(8,128)(2,1)S(1)}, bf16[512,512]{1,0:T(8,128)(2,1)}, u32[]{:S(2)}) copy-start(bf16[512,512]{1,0:T(8,128)(2,1)} %param.16) | copy-start | bytes 1572868
  192.1 7.1 %copy-start.53 = (f32[512]{0:T(512)S(1)}, f32[512]{0:T(512)}, u32[]{:S(2)}) copy-start(f32[512]{0:T(512)} %copy-done.52) | copy-start | bytes 6148
  192.1 7.1 %copy-start.63 = (f32[512]{0:T(512)S(1)}, f32[512]{0:T(512)}, u32[]{:S(2)}) copy-start(f32[512]{0:T(512)} %param.20) | copy-start | bytes 6148
  192.1 7.6 %copy-start.59 = (f32[512]{0:T(512)S(1)}, f32[512]{0:T(512)}, u32[]{:S(2)}) copy-start(f32[512]{0:T(512)} %copy-done.58) | copy-start | bytes 6148
  192.1 7.6 %copy-start.57 = (f32[512]{0:T(512)S(1)}, f32[512]{0:T(512)}, u32[]{:S(2)}) copy-start(f32[512]{0:T(512)} %copy-done.56) | copy-start | bytes 6148
  202.0 7.4 %copy-start.46 = (bf16[8,64,512]{2,1,0:T(8,128)(2,1)S(1)}, bf16[8,64,512]{2,1,0:T(8,128)(2,1)}, u32[]{:S(2)}) copy-start(bf16[8,64,512]{2,1,0:T(8,128)(2,1)} %copy-done.45) | copy-start | bytes 1572868
  202.1 8.9 %copy-start.11 = (bf16[512,512]{0,1:T(8,128)(2,1)S(1)}, bf16[512,512]{0,1:T(8,128)(2,1)}, u32[]{:S(2)}) copy-start(bf16[512,512]{0,1:T(8,128)(2,1)} %copy-done.10) | copy-start | bytes 1572868
  202.1 8.9 %copy-start.30 = (bf16[512,8,64]{0,2,1:T(8,128)(2,1)S(1)}, bf16[512,8,64]{0,2,1:T(8,128)(2,1)}, u32[]{:S(2)}) copy-start(bf16[512,8,64]{0,2,1:T(8,128)(2,1)} %copy-done.29) | copy-start | bytes 1572868
  204.2 8.2 %copy-start.24 = (bf16[512,2048]{1,0:T(8,128)(2,1)S(1)}, bf16[512,2048]{1,0:T(8,128)(2,1)}, u32[]{:S(2)}) copy-start(bf16[512,2048]{1,0:T(8,128)(2,1)} %copy-done.23) | copy-start | bytes 6291460
  213.7 4.4 %copy-start.19 = (f32[512,2048]{1,0:T(8,128)S(1)}, f32[512,2048]{1,0:T(8,128)}, u32[]{:S(2)}) copy-start(f32[512,2048]{1,0:T(8,128)} %copy-done.18) | copy-start | bytes 12582916
  213.7 4.4 %copy-start.38 = (bf16[1,512,512]{2,1,0:T(8,128)(2,1)S(1)}, bf16[1,512,512]{2,1,0:T(8,128)(2,1)}, u32[]{:S(2)}) copy-start(bf16[1,512,512]{2,1,0:T(8,128)(2,1)} %param.25) | copy-start | bytes 1572868
  218.2 3.9 %copy-start.74 = (f32[512]{0:T(512)S(1)}, f32[512]{0:T(512)}, u32[]{:S(2)}) copy-start(f32[512]{0:T(512)} %get-tuple-element.34) | copy-start | bytes 6148
  337.6 7.6 %copy-start.1 = (bf16[512,2048]{1,0:T(8,128)(2,1)S(1)}, bf16[512,2048]{1,0:T(8,128)(2,1)}, u32[]{:S(2)}) copy-start(bf16[512,2048]{1,0:T(8,128)(2,1)} %param.18) | copy-start | bytes 6291460
  340.0 4.6 %copy-start.75 = (f32[8,128]{1,0:T(8,128)S(1)}, f32[8,128]{1,0:T(8,128)}, u32[]{:S(2)}) copy-start(f32[8,128]{1,0:T(8,128)} %get-tuple-element.13) | copy-start | bytes 12292
  (34 other events, 76.4 us)

commit v2 on v0

v2 whole, which is shorter than its diff:
```python
import functools
import math

import jax
import jax.numpy as jnp
from jax import lax
from jax.experimental import pallas as pl
from jax.experimental.pallas import tpu as pltpu
from jax.sharding import PartitionSpec as P

MESH = pl.DeviceIdType.MESH
F32, BF16 = jnp.float32, jnp.bfloat16
T, D, H, DH, M, FF = 512, 512, 8, 64, 256, 2048
SLAB = 136
DIM_ORDER = (0, 2, 4, 1, 3, 5)
EPS = 1e-05
C = DH ** -0.25
ALPHA = C * math.log2(math.e)
GELU_A, GELU_B = math.sqrt(2.0 / math.pi), 0.044715


def dot(a, b):
    return lax.dot_general(a, b, (((1,), (0,)), ((), ())), preferred_element_type=F32)


def dot_nt(a, b):
    return lax.dot_general(a, b, (((1,), (1,)), ((), ())), preferred_element_type=F32)


def dot_tn(a, b):
    return lax.dot_general(a, b, (((0,), (0,)), ((), ())), preferred_element_type=F32)


def iota(shape, dim):
    return lax.broadcasted_iota(jnp.int32, shape, dim)


def place():
    pack, seq = lax.axis_index("pack"), lax.axis_index("seq")
    return pack // 2, pack % 2, seq // 4, seq % 4


def neighbour(dim, z, core, x, y):
    axis = dim // 2
    here = (x, y, z)[axis]
    if dim % 2 == 0:
        there, side = here + 1 - 2 * (here % 2), ((here + 1) // 2) % 2
    else:
        there, side = 3 - here, here // 2
    x = there if axis == 0 else x
    y = there if axis == 1 else y
    z = there if axis == 2 else z
    return (z * 2 + core, x * 4 + y), side


def layer_norm(v):
    centred = v - jnp.mean(v, axis=-1, keepdims=True)
    scale = lax.rsqrt(jnp.mean(centred * centred, axis=-1, keepdims=True) + EPS)
    return centred * scale, scale


def norm_back(n, scale, e):
    return scale * (e - jnp.mean(e, axis=-1, keepdims=True) - n * jnp.mean(e * n, axis=-1, keepdims=True))


def row_loop(step, body, carry=0):
    def run(i, c):
        return body(pl.ds(pl.multiple_of(i * step, step), step), c)

    return lax.fori_loop(0, T // step, run, carry)


def head_loop(body):
    def run(h, c):
        body(h)
        return c

    lax.fori_loop(0, H, run, 0)


class Job:
    def __init__(self, r, where, color, sem, row, lane, width, rows=1024):
        self.r, self.where, self.color, self.sem = r, where, color, sem
        self.row, self.lane, self.width = row, lane, width
        self.n = rows // 2
        self.off = row + where[1] * self.n
        self.step = -1

    def part(self, row, count):
        return self.r.g.at[pl.ds(pl.multiple_of(row, 8), count), pl.ds(self.lane, self.width)]

    def copy(self, src, dst, dev):
        self.now = pltpu.make_async_remote_copy(
            src_ref=src, dst_ref=dst, send_sem=self.r.ssem.at[self.sem, self.step], recv_sem=self.r.rsem.at[self.sem, self.step],
            device_id=dev, device_id_type=MESH)
        self.now.start()

    def add(self, buf, buf_row, count):
        r, lanes, step = self.r, pl.ds(self.lane, self.width), min(64, count)

        def body(i, c):
            at = pl.ds(pl.multiple_of(self.off + i * step, 8), step)
            r.g[at, lanes] += buf[pl.ds(pl.multiple_of(buf_row + i * step, 8), step), lanes]
            return c

        lax.fori_loop(0, count // step, body, 0)

    def tick(self):
        z, core, x, y = self.where
        r, n, lanes = self.r, self.n, pl.ds(self.lane, self.width)
        base = self.row // 2
        sibling = (z * 2 + 1 - core, x * 4 + y)
        s = self.step
        link = lambda k: neighbour(DIM_ORDER[(k + self.color) % 6], z, core, x, y)
        if s >= 0:
            self.now.wait()
        if s == 0:
            pl.semaphore_signal(r.free.at[self.sem, 6], inc=1, device_id=sibling, device_id_type=MESH)
            self.add(r.from_core, base, n)
        elif 1 <= s <= 6:
            dev, side = link(s - 1)
            h = n >> s
            if s < 6:
                pl.semaphore_signal(r.free.at[self.sem, s - 1], inc=1, device_id=dev, device_id_type=MESH)
            self.off = self.off + side * h
            self.add(r.from_chip, base + n - 2 * h, h)
        elif 7 <= s <= 12:
            k = 12 - s
            dev, side = link(k)
            h = n >> (k + 1)
            if k == 5:
                r.g[pl.ds(pl.multiple_of(self.off + (1 - 2 * side) * h, 8), h), lanes] = r.turn[self.sem // 4, :, pl.ds(self.lane if self.width < 512 else 0, self.width)]
            self.off = self.off - side * h
        self.step = s = s + 1
        if s == 0:
            self.copy(self.part(self.row + (1 - core) * n, n), r.from_core.at[pl.ds(base, n), lanes], sibling)
        elif s <= 6:
            dev, side = link(s - 1)
            h = n >> s
            self.copy(self.part(self.off + (1 - side) * h, h), r.from_chip.at[pl.ds(base + n - 2 * h, h), lanes], dev)
        elif s <= 12:
            k = 12 - s
            dev, side = link(k)
            h = n >> (k + 1)
            part = self.part(self.off, h)
            if k == 5:
                self.copy(part, r.turn.at[self.sem // 4, :, pl.ds(self.lane if self.width < 512 else 0, self.width)], dev)
            else:
                pl.semaphore_wait(r.free.at[self.sem, k], 1)
                self.copy(part, part, dev)
        elif s == 13:
            pl.semaphore_wait(r.free.at[self.sem, 6], 1)
            part = self.part(self.off, n)
            self.copy(part, part, sibling)


class Exchange:
    def __init__(self, r, which, pack, seq):
        self.r, self.sems, self.pack, self.seq = r, r.esem.at[which], pack, seq

    def send(self, src, dst, way):
        copies = []
        for step in range(1, 16):
            peer = lax.rem(self.seq + step, 16)
            copy = pltpu.make_async_remote_copy(
                src_ref=src.at[peer], dst_ref=dst.at[self.seq],
                send_sem=self.sems.at[2 * way, step - 1], recv_sem=self.sems.at[2 * way + 1, step - 1],
                device_id=(self.pack, peer), device_id_type=MESH)
            copy.start()
            copies.append(copy)
        dst[self.seq] = src[self.seq]
        self.copies = copies

    def wait(self):
        for copy in self.copies:
            copy.wait()

    def begin(self):
        self.send(self.r.out, self.r.arrived, 0)

    def turn(self):
        self.wait()
        arrived, back = self.r.arrived, self.r.back

        def left(dev, carry):
            total, small = carry
            tail, mine = arrived[dev - 1, 128:136], arrived[dev, 128:136]
            whole = tail[2:3] == tail[3:4]
            joins = tail[3:4] == mine[2:3]
            total = jnp.where(joins, arrived[dev - 1, 64:128] + jnp.where(whole, total, 0.0), 0.0)
            small = jnp.where(joins, tail[1:2] + jnp.where(whole, small, 0.0), 0.0)
            back[dev, 0:64] = total
            back[dev, 128:129] = small
            return total, small

        def right(i, carry):
            dev = 14 - i
            total, small = carry
            tail, mine = arrived[dev + 1, 128:136], arrived[dev, 128:136]
            whole = tail[2:3] == tail[3:4]
            joins = mine[3:4] == tail[2:3]
            total = jnp.where(joins, arrived[dev + 1, 0:64] + jnp.where(whole, total, 0.0), 0.0)
            small = jnp.where(joins, tail[0:1] + jnp.where(whole, small, 0.0), 0.0)
            back[dev, 64:128] = total
            back[dev, 129:130] = small
            return total, small

        none = (jnp.zeros((64, 128), F32), jnp.zeros((1, 128), F32))
        for dev in range(16):
            back[dev, 128:136] = jnp.zeros((8, 128), F32)
        back[0, 0:64] = none[0]
        back[15, 64:128] = none[0]
        lax.fori_loop(1, 16, left, none)
        lax.fori_loop(0, 15, right, none)
        self.send(back, self.r.got, 1)


class Gains:
    def __init__(self, r, pack, seq):
        self.r, self.pack, self.seq = r, pack, seq

    def send(self, src, dst, way, size):
        self.copies = []
        for step in range(1, size):
            dev = (lax.rem(self.pack + step, 8), self.seq) if way == 0 else (self.pack, lax.rem(self.seq + step, 16))
            copy = pltpu.make_async_remote_copy(
                src_ref=src, dst_ref=dst.at[step - 1], send_sem=self.r.gsem.at[2 * way, step - 1],
                recv_sem=self.r.gsem.at[2 * way + 1, step - 1], device_id=dev, device_id_type=MESH)
            copy.start()
            self.copies.append(copy)

    def begin(self):
        self.send(self.r.gain_here, self.r.gain_pack, 0, 8)

    def turn(self):
        for copy in self.copies:
            copy.wait()
        total = self.r.gain_here[...]
        for i in range(7):
            total = total + self.r.gain_pack[i]
        self.r.gain_mid[...] = total
        self.send(self.r.gain_mid, self.r.gain_seq, 1, 16)

    def end(self):
        for copy in self.copies:
            copy.wait()
        total = self.r.gain_mid[...]
        for i in range(15):
            total = total + self.r.gain_seq[i]
        return total


class Refs:
    pass


SCRATCH = [
    ("x", (T, D), BF16), ("cot", (T, D), BF16),
    ("wqkv", (3, D, D), BF16), ("wo", (D, D), BF16),
    ("wup", (4, D, 512), BF16), ("wdown", (4, 512, D), BF16), ("rf", (H, DH, M), BF16),
    ("rx", (4, 256, 512), BF16), ("r80", (H, 80, M), BF16),
    ("nb", (T, D), BF16), ("nT", (D, T), BF16), ("qT", (D, T), BF16), ("kT", (D, T), BF16),
    ("xb", (4, T, 512), BF16),
    ("gup", (4, T, 512), BF16),
    ("vext", (H, 80, T), BF16), ("gext", (H, 80, T), BF16),
    ("phik", (H, T, M), BF16), ("phiq", (H, T, M), BF16),
    ("dcol", (T, T), F32),
    ("num", (H, DH, T), F32), ("den", (H, 8, T), F32),
    ("attT", (D, T), BF16), ("att", (T, D), BF16), ("mid", (T, D), F32), ("hid", (T, D), BF16), ("hidT", (D, T), BF16),
    ("acc", (T, D), F32), ("acc2", (T, D), F32), ("gmid", (T, D), F32), ("gb", (T, D), BF16),
    ("sb1", (H, 144, M), BF16), ("sb2", (H, 144, M), BF16),
    ("gvT", (H, DH, T), F32), ("gT", (3, D, T), BF16),
    ("obf", (T, D), BF16), ("gibf", (T, D), BF16),
    ("out", (16, SLAB, 128), F32), ("arrived", (16, SLAB, 128), F32), ("back", (16, SLAB, 128), F32), ("got", (16, SLAB, 128), F32),
    ("g", (6144, 512), F32), ("from_core", (3072, 512), F32), ("from_chip", (3072, 512), F32), ("turn", (6, 8, 512), F32),
    ("gain_sum", (2, 8, D), F32), ("gain_here", (8, 128), F32), ("gain_pack", (7, 8, 128), F32), ("gain_mid", (8, 128), F32), ("gain_seq", (15, 8, 128), F32),
]
SEMS = [
    ("load", pltpu.SemaphoreType.DMA((20,))), ("store", pltpu.SemaphoreType.DMA((16,))),
    ("esem", pltpu.SemaphoreType.DMA((2, 4, 15))), ("gsem", pltpu.SemaphoreType.DMA((4, 15))),
    ("ssem", pltpu.SemaphoreType.DMA((24, 14))), ("rsem", pltpu.SemaphoreType.DMA((24, 14))),
    ("free", pltpu.SemaphoreType.REGULAR((24, 7))),
]
ROW_DOWN, ROW_UP, ROW_O, ROW_Q, ROW_K, ROW_V = 0, 2048, 4096, 4608, 5120, 5632


def kernel(
    x_h, wq_h, wk_h, wv_h, wo_h, wup_h, wdown_h, rf_h, cot_h, ga_ref, gf_ref, doc_ref, live_ref,
    out_h, gin_h, gwq_h, gwk_h, gwv_h, gwo_h, gwup_h, gwdown_h, gain_ref, *scratch):
    r = Refs()
    for (name, *_), ref in zip(SCRATCH + SEMS, scratch):
        setattr(r, name, ref)
    where = place()
    z, core, px, py = where
    pack, seq = lax.axis_index("pack"), lax.axis_index("seq")

    loads = {}

    def load(name, src, dst):
        copy = pltpu.make_async_copy(src, dst, r.load.at[len(loads)])
        copy.start()
        loads[name] = copy

    load("x", x_h, r.x)
    load("wk", wk_h, r.wqkv.at[1])
    load("wv", wv_h, r.wqkv.at[2])
    load("rf", rf_h, r.rf)
    load("wq", wq_h, r.wqkv.at[0])
    load("wo", wo_h, r.wo)
    for j in range(4):
        load("wup%d" % j, wup_h.at[:, pl.ds(j * 512, 512)], r.wup.at[j])
    load("cot", cot_h, r.cot)
    for j in range(4):
        load("wdown%d" % j, wdown_h.at[pl.ds(j * 512, 512)], r.wdown.at[j])
    barrier = pltpu.get_barrier_semaphore()
    for step in range(1, 16):
        pl.semaphore_signal(barrier, inc=1, device_id=(pack, lax.rem(seq + step, 16)), device_id_type=MESH)
    for step in range(1, 8):
        pl.semaphore_signal(barrier, inc=1, device_id=(lax.rem(pack + step, 8), seq), device_id_type=MESH)

    doc = doc_ref[...].astype(F32)
    doc_f, doc_l = doc[:, 0:1], doc[:, T - 1:T]
    in_f, in_l = doc == doc_f, doc == doc_l
    one_f, one_l = in_f.astype(F32), in_l.astype(F32)
    row16 = iota((16, T), 0)

    def ends(block, tail_f, tail_l):
        zero = jnp.zeros_like(block)
        tail = jnp.where(row16 == 0, tail_f, jnp.where(row16 == 1, tail_l, 0.0))
        return jnp.concatenate(
            [jnp.where(in_f, block, zero).astype(BF16), jnp.where(in_l, block, zero).astype(BF16), tail.astype(BF16)], axis=0)

    dcol = jnp.broadcast_to(doc, (128, T)).T
    for j in range(4):
        r.dcol[:, j * 128:(j + 1) * 128] = dcol
    live = jnp.broadcast_to(live_ref[...].astype(F32), (128, T)).T

    loads["x"].wait()

    def first_norm(rows, c):
        n, _ = layer_norm(r.x[rows, :].astype(F32))
        r.nb[rows, :] = (n * ga_ref[...]).astype(BF16)
        return c

    row_loop(64, first_norm)
    loads["rf"].wait()
    for p in range(4):
        lane, row = iota((256, 512), 1) // 256, iota((256, 512), 0)
        pick = (row >= 128) & (row < 152) & (row % 8 == 2 * p + lane)
        r.rx[p] = jnp.where(pick, 1.0, 0.0).astype(BF16)
        r.rx[p, 0:64, 0:256] = r.rf[2 * p]
        r.rx[p, 64:128, 256:512] = r.rf[2 * p + 1]
    for h in range(H):
        r.r80[h, 0:64] = r.rf[h]
        r.r80[h, 64:80] = jnp.where(iota((16, M), 0) == 0, 1.0, 0.0).astype(BF16)
    pick_heads = ((iota((D, 128), 1) % 8 == iota((D, 128), 0) // DH) & (iota((D, 128), 1) < 24)).astype(BF16)

    def features(w, low, transposed, phi, off, alive):
        flat = dot(r.nb[...], r.wqkv[w]).astype(BF16)
        transposed[...] = flat.T
        square = flat.astype(F32)
        square = square * square
        high = square.astype(BF16)
        rest = (square - high.astype(F32)).astype(BF16)
        size = dot(high, pick_heads) + dot(rest, pick_heads)
        shift = size * (-0.5 * C) - 4.0 / ALPHA
        if alive is not None:
            shift = shift + (alive - 1.0) * 1e30
        first = shift.astype(BF16).astype(F32)
        second = (shift - first).astype(BF16).astype(F32)
        third = shift - first - second
        at = iota((T, 128), 1)
        shift = jnp.where(at < 8, first, jnp.where(at < 16, second, jnp.where(at < 24, third, 0.0))).astype(BF16)
        for p in range(4):
            low[p, :, off:off + 128] = flat[:, p * 128:(p + 1) * 128]
            low[p, :, off + 128:off + 256] = shift

        def one_pair(p, c):
            y = dot(low[p, :, off:off + 256], r.rx[p])
            y = jnp.exp2(y * ALPHA).astype(BF16)
            phi[2 * p] = y[:, 0:256]
            phi[2 * p + 1] = y[:, 256:512]
            return c

        lax.fori_loop(0, 4, one_pair, 0)

    loads["wk"].wait()
    features(1, r.xb, r.kT, r.phik, 0, live)
    loads["wv"].wait()
    vT = dot(r.nb[...], r.wqkv[2]).astype(BF16).T
    for h in range(H):
        r.vext[h, 0:64] = vT[h * 64:(h + 1) * 64]
        r.vext[h, 64:80] = jnp.where(row16 == 0, 1.0, 0.0).astype(BF16)

    def put_slab(h, lhs, phi):
        s = dot(lhs, phi)
        row = iota((8, M), 0)
        tail = jnp.where(row == 2, doc_f, jnp.where(row == 3, doc_l, s[128:136]))
        for half in range(2):
            r.out[2 * h + half, 0:128] = s[0:128, half * 128:(half + 1) * 128]
            r.out[2 * h + half, 128:136] = tail[:, half * 128:(half + 1) * 128]

    def take_slab(h, sb):
        for half in range(2):
            lanes = pl.ds(half * 128, 128)
            sb[h, 0:128, lanes] = r.got[2 * h + half, 0:128].astype(BF16)
            sb[h, 128:144, lanes] = jnp.concatenate(
                [r.got[2 * h + half, 128:136], jnp.zeros((8, 128), F32)], axis=0).astype(BF16)

    def value_ends(h):
        return ends(r.vext[h, 0:64].astype(F32), one_f, one_l)

    head_loop(lambda h: put_slab(h, value_ends(h), r.phik[h]))
    pl.semaphore_wait(barrier, 22)
    exchange = Exchange(r, 0, pack, seq)
    exchange.begin()

    r.nT[...] = r.nb[...].T
    loads["wq"].wait()
    features(0, r.xb, r.qT, r.phiq, 256, None)
    exchange.turn()

    def same(block):
        return jnp.where(r.dcol[...] == doc, block, 0.0).astype(BF16)

    def attend(h):
        local = dot_nt(r.vext[h], same(dot_nt(r.phiq[h], r.phik[h])))
        r.num[h] = local[0:64]
        r.den[h] = local[64:72]

    head_loop(attend)
    exchange.wait()

    def join(h):
        take_slab(h, r.sb1)
        far = dot_nt(r.sb1[h], r.phiq[h])
        num = r.num[h] + jnp.where(in_f, far[0:64], 0.0) + jnp.where(in_l, far[64:128], 0.0)
        den = r.den[h, 0:1] + jnp.where(in_f, far[128:129], 0.0) + jnp.where(in_l, far[129:130], 0.0)
        inv = 1.0 / den
        att = num * inv
        r.num[h] = att
        r.den[h, 0:1] = inv
        r.attT[pl.ds(pl.multiple_of(h * 64, 64), 64)] = att.astype(BF16)

    head_loop(join)
    r.att[...] = r.attT[...].T
    loads["wo"].wait()
    r.mid[...] = dot(r.att[...], r.wo[...])

    def second_norm(rows, c):
        mid = r.x[rows, :].astype(F32) + r.mid[rows, :]
        r.mid[rows, :] = mid
        n, _ = layer_norm(mid)
        r.hid[rows, :] = (n * gf_ref[...]).astype(BF16)
        return c

    row_loop(64, second_norm)

    loads["cot"].wait()
    for j in range(4):
        loads["wup%d" % j].wait()
        loads["wdown%d" % j].wait()

    def feed(j, c):
        r.acc[...] = dot(r.hid[...], r.wup[j])
        r.acc2[...] = dot_nt(r.cot[...], r.wdown[j])

        def gelu(rows, c):
            u = r.acc[rows, :]
            ga = r.acc2[rows, :].astype(BF16).astype(F32)
            sq = u * u
            t = jnp.tanh(u * (GELU_A + GELU_A * GELU_B * sq))
            half = 0.5 * (1.0 + t)
            slope = half + 0.5 * u * (1.0 - t * t) * (GELU_A + 3.0 * GELU_A * GELU_B * sq)
            r.xb[j, rows, :] = (u * half).astype(BF16)
            r.gup[j, rows, :] = (ga * slope).astype(BF16)
            return c

        row_loop(16, gelu)
        back = dot_nt(r.gup[j], r.wup[j])

        @pl.when(j == 0)
        def _():
            r.gmid[...] = back

        @pl.when(j > 0)
        def _():
            r.gmid[...] += back

        return c

    lax.fori_loop(0, 4, feed, 0)

    def add_gain(which, p):
        total = r.gain_sum[which]
        for i in range(8):
            total = total + p[i * 8:(i + 1) * 8]
        r.gain_sum[which] = total

    r.gain_sum[...] = jnp.zeros((2, 8, D), F32)

    def second_back(rows, c):
        gh = r.gmid[rows, :].astype(BF16).astype(F32)
        n, scale = layer_norm(r.mid[rows, :])
        gm = r.cot[rows, :].astype(F32) + norm_back(n, scale, gh * gf_ref[...])
        r.gmid[rows, :] = gm
        r.gb[rows, :] = gm.astype(BF16)
        add_gain(1, gh * n)
        return c

    row_loop(64, second_back)
    r.acc[...] = dot_nt(r.wo[...], r.gb[...])

    def gates(h):
        ga = r.acc[pl.ds(pl.multiple_of(h * 64, 64), 64)].astype(BF16).astype(F32)
        inv = r.den[h, 0:1]
        gn = (ga * inv).astype(BF16)
        gd = -jnp.sum(ga * r.num[h], axis=0, keepdims=True) * inv
        r.gext[h, 0:64] = gn
        r.gext[h, 64:80] = jnp.where(row16 == 0, gd, 0.0).astype(BF16)
        put_slab(h, grad_ends(h), r.phiq[h])

    def grad_ends(h):
        gd = r.gext[h, 64:80].astype(F32)[0:1]
        return ends(r.gext[h, 0:64].astype(F32), one_f * gd, one_l * gd)

    head_loop(gates)
    exchange = Exchange(r, 1, pack, seq)
    exchange.begin()

    jobs = [Job(r, where, k, 4 * k, k * 1024, 0, 512) for k in range(5)]

    def block(row, value):
        r.g[row:row + 512, :] = value

    for k in range(2):
        for j in range(2 * k, 2 * k + 2):
            block(ROW_DOWN + j * 512, dot_tn(r.xb[j], r.cot[...]))
        jobs[k].tick()
    r.hidT[...] = r.hid[...].T
    for k in range(2):
        for j in range(2 * k, 2 * k + 2):
            block(ROW_UP + j * 512, dot(r.hidT[...], r.gup[j]))
        jobs[2 + k].tick()
    for job in jobs[0:2]:
        job.tick()
    block(ROW_O, dot(r.attT[...], r.gb[...]))
    for job in jobs[2:4]:
        job.tick()
    exchange.turn()

    def map_back(h, gphi, phi, flat, which):
        p = (gphi.astype(BF16).astype(F32) * phi.astype(F32)).astype(BF16)
        through = dot_nt(r.r80[h], p)
        rows = pl.ds(pl.multiple_of(h * 64, 64), 64)
        r.gT[which, rows] = (C * through[0:64] - (C * C) * through[64:65] * flat[rows].astype(F32)).astype(BF16)

    def query_back(h):
        gphi = dot(same(dot_tn(r.gext[h], r.vext[h])), r.phik[h]) + dot_tn(grad_ends(h), r.sb1[h])
        map_back(h, gphi, r.phiq[h], r.qT, 0)
        r.gvT[h] = dot(r.gext[h, 0:64], same(dot_nt(r.phiq[h], r.phik[h])))

    head_loop(query_back)
    block(ROW_Q, dot_nt(r.nT[...], r.gT[0]))
    jobs[4].tick()
    for job in jobs[0:4]:
        job.tick()
    stores = []

    def store(src, dst):
        copy = pltpu.make_async_copy(src, dst, r.store.at[len(stores)])
        copy.start()
        stores.append(copy)

    r.acc[...] = dot(r.xb[0], r.wdown[0])
    for j in range(1, 4):
        r.acc[...] += dot(r.xb[j], r.wdown[j])

    def put_out(rows, c):
        r.obf[rows, :] = (r.mid[rows, :] + r.acc[rows, :]).astype(BF16)
        return c

    row_loop(64, put_out)
    store(r.obf, out_h)
    for job in jobs:
        job.tick()
    exchange.wait()

    def key_back(h):
        take_slab(h, r.sb2)
        gphi = dot(same(dot_tn(r.vext[h], r.gext[h])), r.phiq[h]) + dot_tn(value_ends(h), r.sb2[h])
        map_back(h, gphi, r.phik[h], r.kT, 1)
        far = dot_nt(r.sb2[h, 0:128], r.phik[h])
        rows = pl.ds(pl.multiple_of(h * 64, 64), 64)
        r.gT[2, rows] = (r.gvT[h] + jnp.where(in_f, far[0:64], 0.0) + jnp.where(in_l, far[64:128], 0.0)).astype(BF16)

    head_loop(key_back)
    block(ROW_K, dot_nt(r.nT[...], r.gT[1]))
    block(ROW_V, dot_nt(r.nT[...], r.gT[2]))
    last = [Job(r, where, k + 1, 20 + k, 5120, k * 128, 128) for k in range(4)]
    for job in last + jobs:
        job.tick()
    r.acc2[...] = dot(r.wqkv[0], r.gT[0])

    def normed_back(i, c):
        r.acc2[...] += dot(r.wqkv[i], r.gT[i])
        return c

    lax.fori_loop(1, 3, normed_back, 0)
    r.acc[...] = r.acc2[...].T
    for job in last + jobs:
        job.tick()

    def first_back(rows, c):
        gn = r.acc[rows, :].astype(BF16).astype(F32)
        n, scale = layer_norm(r.x[rows, :].astype(F32))
        r.gibf[rows, :] = (r.gmid[rows, :] + norm_back(n, scale, gn * ga_ref[...])).astype(BF16)
        add_gain(0, gn * n)
        return c

    row_loop(64, first_back)
    store(r.gibf, gin_h)
    for which in range(2):
        total = r.gain_sum[which, 0:1]
        for i in range(1, 8):
            total = total + r.gain_sum[which, i:i + 1]
        for j in range(4):
            r.gain_here[4 * which + j:4 * which + j + 1] = total[:, j * 128:(j + 1) * 128]
    gains = Gains(r, pack, seq)
    gains.begin()
    for job in last + jobs:
        job.tick()
    gains.turn()
    while last[0].step < 13 or jobs[4].step < 13:
        for job in last + jobs:
            if job.step < 13:
                job.tick()
    gain_ref[...] = gains.end()
    for job in jobs + last:
        job.now.wait()
    for j in range(4):
        store(r.g.at[pl.ds(ROW_DOWN + j * 512, 512)], gwdown_h.at[pl.ds(j * 512, 512)])
        store(r.g.at[pl.ds(ROW_UP + j * 512, 512)], gwup_h.at[:, pl.ds(j * 512, 512)])
    for row, dst in ((ROW_O, gwo_h), (ROW_Q, gwq_h), (ROW_K, gwk_h), (ROW_V, gwv_h)):
        store(r.g.at[pl.ds(row, 512)], dst)
    for copy in stores:
        copy.wait()


def per_device(
    inputs, w_query, w_key, w_value, w_output, w_up, w_down, gain_attn, gain_ffn, random_features, doc_ids, live_rows, cotangent):
    any_space = pl.BlockSpec(memory_space=pl.ANY)
    vmem = pl.BlockSpec(memory_space=pltpu.VMEM)
    f32 = lambda *shape: jax.ShapeDtypeStruct(shape, F32)
    low = jax.ShapeDtypeStruct((T, D), BF16)
    outs = pl.pallas_call(
        kernel,
        out_shape=(low, low, f32(D, D), f32(D, D), f32(D, D), f32(D, D), f32(D, FF), f32(FF, D), f32(8, 128)),
        in_specs=[any_space] * 9 + [vmem] * 4,
        out_specs=(any_space,) * 8 + (vmem,),
        scratch_shapes=[pltpu.VMEM(shape, dtype) for _, shape, dtype in SCRATCH] + [sem for _, sem in SEMS],
        compiler_params=pltpu.CompilerParams(collective_id=0, has_side_effects=True, vmem_limit_bytes=63 * 2**20),
    )(
        inputs[0], w_query, w_key, w_value, w_output, w_up, w_down, random_features, cotangent[0],
        gain_attn[None], gain_ffn[None], doc_ids, live_rows)
    gain = outs[8].reshape(2 * D)
    return (outs[0][None], outs[1][None]) + tuple(outs[2:8]) + (gain[:D], gain[D:])


def solution(mesh):
    rows = P("pack", "seq", None)
    return jax.shard_map(
        per_device,
        mesh=mesh,
        in_specs=(rows,) + (P(),) * 9 + (P("pack", "seq"), P("pack", "seq"), rows),
        out_specs=(rows, rows) + (P(),) * 8,
        check_vma=False,
    )
```

time: 528 us -> 228 us (0.43); the launches traced: 520 us -> 228 us
  waiting for transfers between devices: 300 us -> 0 us
  Pallas kernels: 0 us -> 211 us
  matrix products: 89.4 us -> 0 us
  blocking collectives: 65.7 us -> 0 us
  other arithmetic: 17 us -> 0 us
  local copies, waits for them, and re-layouts: 33.1 us -> 16.3 us
  between operations: 14.8 us -> 0.68 us
    psum x3 -> x0, waiting for transfers between devices: 300 us -> none  [the longest x1 111 us: per_device(): summed_docs, summed_tots = lax.psum((local_summary, local_totals), 'seq')]
    pallas_call x0 -> x1, Pallas kernels: none -> 211 us  [per_device(): pl.pallas_call(kernel, out_shape=(low, low, f32(D, D), f32(D, D), f32(D,...]
    dot_general x32 -> x0, matrix products: 89.4 us -> none  [the longest x12 20.9 us: contract(): lax.dot_general(left_side, right_side, (((left_dim,), (right_dim,)), ((),...]
    psum x1 -> x0, blocking collectives: 65.7 us -> none  [per_device(): lax.psum((grad_w_query, grad_w_key, grad_w_value, grad_w_output, grad_w_u...]
    convert_element_type x7 -> x0, other arithmetic: 15.3 us -> none  [the longest x1 7.02 us: per_device(): summary_low = summary.astype(jnp.bfloat16)]
    unnamed x118 -> x18, local copies, waits for them, and re-layouts: 25.1 us -> 14.9 us
    convert_element_type x2 -> x0, local copies, waits for them, and re-layouts: 7.96 us -> none  [the longest x1 4.06 us: per_device(): phi_query = phi_query_float.astype(jnp.bfloat16)]
  transfers between devices with their start and end apart: 3 -> 0, of which waited for: 3 -> 0; matrix products, arithmetic and copies ran while one was open for 7% -> 0% of each run, Pallas kernels for 0% -> 0%
where the time goes in v2:
time: 228 us
  Pallas kernels  211 us (93%)
  local copies, waits for them, and re-layouts  16.3 us (7%)
    pallas_call x1, Pallas kernels, per_device(): pl.pallas_call(kernel, out_shape=(low, low, f32(D, D), f32(D, D), f32(D,...  211 us
    unnamed x18, local copies, waits for them, and re-layouts  14.9 us

profile of v2, /device:TPU:1, one launch (start us, length us, event | category | flops | bytes accessed | tf_op | source)
XLA Modules:
  0.0 228.1 jit_solution(5980937200453438841)
XLA Ops:
  0.6 211.1 %shard_map.204 = (bf16[512,512]{1,0:T(8,128)(2,1)}, bf16[512,512]{1,0:T(8,128)(2,1)}, f32[512,512]{1,0:T(8,128)}, f32[512,512]{1,0:T(8,128)}, f32[512,512]{1,0:T...) custom-call(bf16[512,512]{1,0:T(8,128)(2,1)} %bitcast.10, ...), custom_call_target="tpu_custom_call" | custom-call | tf_op jit(solution)/shard_map/pallas_call | solution.py:656
  211.8 0.0 copy-start.4
  211.8 0.0 copy-start.3
  211.8 1.4 slice_bitcast_fusion
  213.2 0.0 copy-start.2
  213.2 2.0 copy.31
  215.2 1.9 copy.32
  217.0 0.0 copy-start.1
  217.0 2.4 %copy.33 = f32[512,512]{1,0:T(8,128)} copy(f32[512,512]{1,0:T(8,128)} %get-tuple-element.42) | data formatting | bytes 2097152
  219.4 0.0 copy-done.4
  219.4 1.0 copy.34
  220.4 0.0 copy-done.3
  220.4 1.0 copy.35
  221.4 0.0 copy-done.2
  221.4 1.0 copy.36
  222.4 0.0 copy-done.1
  222.4 0.0 copy-start
  222.4 2.1 copy.37
  224.5 1.6 copy-done
  226.1 2.0 copy.38
Async XLA Ops:
  211.8 7.7 %copy-start.4 = (f32[512,512]{1,0:T(8,128)S(1)}, f32[512,512]{1,0:T(8,128)}, u32[]{:S(2)}) copy-start(f32[512,512]{1,0:T(8,128)} %get-tuple-element.43) | copy-start | bytes 3145732
  211.8 8.6 %copy-start.3 = (f32[512,512]{1,0:T(8,128)S(1)}, f32[512,512]{1,0:T(8,128)}, u32[]{:S(2)}) copy-start(f32[512,512]{1,0:T(8,128)} %get-tuple-element.44) | copy-start | bytes 3145732
  213.2 8.2 %copy-start.2 = (f32[512,512]{1,0:T(8,128)S(1)}, f32[512,512]{1,0:T(8,128)}, u32[]{:S(2)}) copy-start(f32[512,512]{1,0:T(8,128)} %get-tuple-element.45) | copy-start | bytes 3145732
  217.0 5.3 %copy-start.1 = (f32[512,2048]{1,0:T(8,128)S(1)}, f32[512,2048]{1,0:T(8,128)}, u32[]{:S(2)}) copy-start(f32[512,2048]{1,0:T(8,128)} %get-tuple-element.46) | copy-start | bytes 12582916
  222.4 3.7 %copy-start = (f32[2048,512]{1,0:T(8,128)S(1)}, f32[2048,512]{1,0:T(8,128)}, u32[]{:S(2)}) copy-start(f32[2048,512]{1,0:T(8,128)} %get-tuple-element.47) | copy-start | bytes 12582916

commit v3 on v2

--- a/solution.py
+++ b/solution.py
@@ -12,8 +12,8 @@
 F32, BF16 = jnp.float32, jnp.bfloat16
 T, D, H, DH, M, FF = 512, 512, 8, 64, 256, 2048
 SLAB = 136
-DIM_ORDER = (0, 2, 4, 1, 3, 5)
 EPS = 1e-05
+VMEM_LIMIT = 46 * 2**20
 C = DH ** -0.25
 ALPHA = C * math.log2(math.e)
 GELU_A, GELU_B = math.sqrt(2.0 / math.pi), 0.044715
@@ -38,19 +38,6 @@
 def place():
     pack, seq = lax.axis_index("pack"), lax.axis_index("seq")
     return pack // 2, pack % 2, seq // 4, seq % 4
-
-
-def neighbour(dim, z, core, x, y):
-    axis = dim // 2
-    here = (x, y, z)[axis]
-    if dim % 2 == 0:
-        there, side = here + 1 - 2 * (here % 2), ((here + 1) // 2) % 2
-    else:
-        there, side = 3 - here, here // 2
-    x = there if axis == 0 else x
-    y = there if axis == 1 else y
-    z = there if axis == 2 else z
-    return (z * 2 + core, x * 4 + y), side
 
 
 def layer_norm(v):
@@ -70,88 +57,144 @@
     return lax.fori_loop(0, T // step, run, carry)
 
 
-def head_loop(body):
+def head_loop(body, start=0, stop=H):
     def run(h, c):
         body(h)
         return c
 
-    lax.fori_loop(0, H, run, 0)
-
-
-class Job:
-    def __init__(self, r, where, color, sem, row, lane, width, rows=1024):
-        self.r, self.where, self.color, self.sem = r, where, color, sem
-        self.row, self.lane, self.width = row, lane, width
-        self.n = rows // 2
-        self.off = row + where[1] * self.n
+    lax.fori_loop(start, stop, run, 0)
+
+
+class Wave:
+    def __init__(self, r, where, row, parts, first):
+        self.parts = []
+        for k, rows in enumerate(parts):
+            self.parts.append(Part(r, where, row, rows // 2, k, first + k))
+            row += rows
+        self.done = False
+
+    def tick(self):
+        if self.done:
+            return
+        for part in self.parts:
+            part.finish()
+            part.start()
+        self.done = self.parts[0].step == 8
+
+
+class Part:
+    def __init__(self, r, where, row, n, color, sem):
+        self.r, self.where, self.row, self.n, self.sem = r, where, row, n, sem
+        self.axes = [(color + i) % 3 for i in range(3)]
+        self.at = row + where[1] * n
+        self.buf = row // 2
         self.step = -1
-
-    def part(self, row, count):
-        return self.r.g.at[pl.ds(pl.multiple_of(row, 8), count), pl.ds(self.lane, self.width)]
-
-    def copy(self, src, dst, dev):
-        self.now = pltpu.make_async_remote_copy(
-            src_ref=src, dst_ref=dst, send_sem=self.r.ssem.at[self.sem, self.step], recv_sem=self.r.rsem.at[self.sem, self.step],
+        self.copies = []
+
+    def peers(self, stage):
+        z, core, x, y = self.where
+        axis = self.axes[stage]
+        mine = (x, y, z)[axis]
+        devs = []
+        for d in range(1, 4):
+            there = (mine + d) % 4
+            x2, y2, z2 = (there if axis == 0 else x), (there if axis == 1 else y), (there if axis == 2 else z)
+            devs.append((there, (z2 * 2 + core, x2 * 4 + y2)))
+        return mine, devs
+
+    def sibling(self):
+        z, core, x, y = self.where
+        return (z * 2 + 1 - core, x * 4 + y)
+
+    def rows(self, at, count):
+        return pl.ds(pl.multiple_of(at, 8), count)
+
+    def lanes(self, quarter):
+        return pl.ds(pl.multiple_of(quarter * 128, 128), 128)
+
+    def send(self, src, dst, dev, d):
+        copy = pltpu.make_async_remote_copy(
+            src_ref=src, dst_ref=dst, send_sem=self.r.ssem.at[self.sem, self.step, d], recv_sem=self.r.rsem.at[self.sem, self.step, d],
             device_id=dev, device_id_type=MESH)
-        self.now.start()
-
-    def add(self, buf, buf_row, count):
-        r, lanes, step = self.r, pl.ds(self.lane, self.width), min(64, count)
+        copy.start()
+        self.copies.append(copy)
+
+    def free(self, stage):
+        for _, dev in self.peers(stage)[1]:
+            pl.semaphore_signal(self.r.free.at[self.sem, stage], inc=1, device_id=dev, device_id_type=MESH)
+
+    def add(self, count, buf, slots):
+        r, step = self.r, min(32, count)
 
         def body(i, c):
-            at = pl.ds(pl.multiple_of(self.off + i * step, 8), step)
-            r.g[at, lanes] += buf[pl.ds(pl.multiple_of(buf_row + i * step, 8), step), lanes]
+            at = self.rows(self.at + i * step, step)
+            total = r.g[at, :]
+            for slot in slots:
+                total = total + buf[self.rows(slot + i * step, step), :]
+            r.g[at, :] = total
             return c
 
         lax.fori_loop(0, count // step, body, 0)
 
-    def tick(self):
-        z, core, x, y = self.where
-        r, n, lanes = self.r, self.n, pl.ds(self.lane, self.width)
-        base = self.row // 2
-        sibling = (z * 2 + 1 - core, x * 4 + y)
-        s = self.step
-        link = lambda k: neighbour(DIM_ORDER[(k + self.color) % 6], z, core, x, y)
-        if s >= 0:
-            self.now.wait()
+    def finish(self):
+        r, n, s = self.r, self.n, self.step
+        for copy in self.copies:
+            copy.wait()
+        self.copies = []
         if s == 0:
-            pl.semaphore_signal(r.free.at[self.sem, 6], inc=1, device_id=sibling, device_id_type=MESH)
-            self.add(r.from_core, base, n)
-        elif 1 <= s <= 6:
-            dev, side = link(s - 1)
-            h = n >> s
-            if s < 6:
-                pl.semaphore_signal(r.free.at[self.sem, s - 1], inc=1, device_id=dev, device_id_type=MESH)
-            self.off = self.off + side * h
-            self.add(r.from_chip, base + n - 2 * h, h)
-        elif 7 <= s <= 12:
-            k = 12 - s
-            dev, side = link(k)
-            h = n >> (k + 1)
-            if k == 5:
-                r.g[pl.ds(pl.multiple_of(self.off + (1 - 2 * side) * h, 8), h), lanes] = r.turn[self.sem // 4, :, pl.ds(self.lane if self.width < 512 else 0, self.width)]
-            self.off = self.off - side * h
-        self.step = s = s + 1
+            pl.semaphore_signal(r.free.at[self.sem, 2], inc=1, device_id=self.sibling(), device_id_type=MESH)
+            self.add(n, r.from_core, [self.buf])
+        elif s in (1, 2):
+            q = n // 4 ** s
+            base = self.buf + (0 if s == 1 else 3 * n // 4)
+            self.free(s - 1)
+            self.at = self.at + self.peers(s - 1)[0] * q
+            self.add(q, r.from_chip, [base + d * q for d in range(3)])
+        elif s == 3:
+            q = n // 16
+            at, mine = self.rows(self.at, q), self.lanes(self.peers(2)[0])
+            buf = pl.ds(self.buf + 15 * n // 16, q)
+            r.g[at, mine] = r.g[at, mine] + r.from_chip[buf, 0:128] + r.from_chip[buf, 128:256] + r.from_chip[buf, 256:384]
+        elif s == 4:
+            q = n // 16
+            at, mine = self.rows(self.at, q), self.peers(2)[0]
+            for d in range(3):
+                r.g[at, self.lanes((mine + 3 - d) % 4)] = r.turn[d, self.buf // 16:self.buf // 16 + q]
+        elif s in (5, 6):
+            q = n // 4 ** (7 - s)
+            self.at = self.at - self.peers(6 - s)[0] * q
+
+    def start(self):
+        r, n = self.r, self.n
+        self.step = s = self.step + 1
         if s == 0:
-            self.copy(self.part(self.row + (1 - core) * n, n), r.from_core.at[pl.ds(base, n), lanes], sibling)
-        elif s <= 6:
-            dev, side = link(s - 1)
-            h = n >> s
-            self.copy(self.part(self.off + (1 - side) * h, h), r.from_chip.at[pl.ds(base + n - 2 * h, h), lanes], dev)
-        elif s <= 12:
-            k = 12 - s
-            dev, side = link(k)
-            h = n >> (k + 1)
-            part = self.part(self.off, h)
-            if k == 5:
-                self.copy(part, r.turn.at[self.sem // 4, :, pl.ds(self.lane if self.width < 512 else 0, self.width)], dev)
-            else:
-                pl.semaphore_wait(r.free.at[self.sem, k], 1)
-                self.copy(part, part, dev)
-        elif s == 13:
-            pl.semaphore_wait(r.free.at[self.sem, 6], 1)
-            part = self.part(self.off, n)
-            self.copy(part, part, sibling)
+            core = self.where[1]
+            self.send(r.g.at[self.rows(self.row + (1 - core) * n, n)], r.from_core.at[pl.ds(self.buf, n)], self.sibling(), 0)
+        elif s in (1, 2):
+            q = n // 4 ** s
+            base = self.buf + (0 if s == 1 else 3 * n // 4)
+            for d, (there, dev) in enumerate(self.peers(s - 1)[1]):
+                self.send(r.g.at[self.rows(self.at + there * q, q)], r.from_chip.at[pl.ds(base + d * q, q)], dev, d)
+        elif s == 3:
+            q = n // 16
+            at = self.rows(self.at, q)
+            for d, (there, dev) in enumerate(self.peers(2)[1]):
+                self.send(r.g.at[at, self.lanes(there)], r.from_chip.at[pl.ds(self.buf + 15 * n // 16, q), pl.ds(d * 128, 128)], dev, d)
+        elif s == 4:
+            q = n // 16
+            mine, devs = self.peers(2)
+            for d, (there, dev) in enumerate(devs):
+                self.send(r.g.at[self.rows(self.at, q), self.lanes(mine)], r.turn.at[d, pl.ds(self.buf // 16, q)], dev, d)
+        elif s in (5, 6):
+            q = n // 4 ** (7 - s)
+            part = r.g.at[self.rows(self.at, q)]
+            pl.semaphore_wait(r.free.at[self.sem, 6 - s], 3)
+            for d, (there, dev) in enumerate(self.peers(6 - s)[1]):
+                self.send(part, part, dev, d)
+        elif s == 7:
+            part = r.g.at[self.rows(self.at, n)]
+            pl.semaphore_wait(r.free.at[self.sem, 2], 1)
+            self.send(part, part, self.sibling(), 0)
 
 
 class Exchange:
@@ -266,30 +309,30 @@
     ("phik", (H, T, M), BF16), ("phiq", (H, T, M), BF16),
     ("dcol", (T, T), F32),
     ("num", (H, DH, T), F32), ("den", (H, 8, T), F32),
-    ("attT", (D, T), BF16), ("att", (T, D), BF16), ("mid", (T, D), F32), ("hid", (T, D), BF16), ("hidT", (D, T), BF16),
-    ("acc", (T, D), F32), ("acc2", (T, D), F32), ("gmid", (T, D), F32), ("gb", (T, D), BF16),
+    ("attT", (D, T), BF16), ("att", (T, D), BF16), ("mid", (T, D), F32), ("hid", (T, D), BF16),
+    ("acc", (T, D), F32), ("acc2", (T, D), F32), ("gmid", (T, D), F32),
     ("sb1", (H, 144, M), BF16), ("sb2", (H, 144, M), BF16),
-    ("gvT", (H, DH, T), F32), ("gT", (3, D, T), BF16),
-    ("obf", (T, D), BF16), ("gibf", (T, D), BF16),
-    ("out", (16, SLAB, 128), F32), ("arrived", (16, SLAB, 128), F32), ("back", (16, SLAB, 128), F32), ("got", (16, SLAB, 128), F32),
-    ("g", (6144, 512), F32), ("from_core", (3072, 512), F32), ("from_chip", (3072, 512), F32), ("turn", (6, 8, 512), F32),
+            ("out", (16, SLAB, 128), F32), ("arrived", (16, SLAB, 128), F32), ("got", (16, SLAB, 128), F32),
+    ("from_core", (3072, 512), F32), ("from_chip", (3072, 512), F32), ("turn", (3, 192, 128), F32),
     ("gain_sum", (2, 8, D), F32), ("gain_here", (8, 128), F32), ("gain_pack", (7, 8, 128), F32), ("gain_mid", (8, 128), F32), ("gain_seq", (15, 8, 128), F32),
 ]
 SEMS = [
-    ("load", pltpu.SemaphoreType.DMA((20,))), ("store", pltpu.SemaphoreType.DMA((16,))),
+    ("load", pltpu.SemaphoreType.DMA((20,))),
     ("esem", pltpu.SemaphoreType.DMA((2, 4, 15))), ("gsem", pltpu.SemaphoreType.DMA((4, 15))),
-    ("ssem", pltpu.SemaphoreType.DMA((24, 14))), ("rsem", pltpu.SemaphoreType.DMA((24, 14))),
-    ("free", pltpu.SemaphoreType.REGULAR((24, 7))),
+    ("ssem", pltpu.SemaphoreType.DMA((9, 8, 3))), ("rsem", pltpu.SemaphoreType.DMA((9, 8, 3))),
+    ("free", pltpu.SemaphoreType.REGULAR((9, 3))),
 ]
 ROW_DOWN, ROW_UP, ROW_O, ROW_Q, ROW_K, ROW_V = 0, 2048, 4096, 4608, 5120, 5632
 
 
 def kernel(
     x_h, wq_h, wk_h, wv_h, wo_h, wup_h, wdown_h, rf_h, cot_h, ga_ref, gf_ref, doc_ref, live_ref,
-    out_h, gin_h, gwq_h, gwk_h, gwv_h, gwo_h, gwup_h, gwdown_h, gain_ref, *scratch):
+    obf, gibf, g, gain_ref, *scratch):
     r = Refs()
+    r.obf, r.gibf, r.g = obf, gibf, g
     for (name, *_), ref in zip(SCRATCH + SEMS, scratch):
         setattr(r, name, ref)
+    r.gb, r.hidT, r.gT, r.back = r.nb, r.att, r.gup, r.out
     where = place()
     z, core, px, py = where
     pack, seq = lax.axis_index("pack"), lax.axis_index("seq")
@@ -487,9 +530,16 @@
         def _():
             r.gmid[...] += back
 
+        r.g[pl.ds(pl.multiple_of(ROW_DOWN + j * 512, 512), 512), :] = dot_tn(r.xb[j], r.cot[...])
         return c
 
     lax.fori_loop(0, 4, feed, 0)
+    waves = [
+        Wave(r, where, ROW_DOWN, (512, 768, 768), 0),
+        Wave(r, where, ROW_UP, (768, 768, 1024), 3),
+        Wave(r, where, ROW_Q, (512, 512, 512), 6),
+    ]
+    waves[0].tick()
 
     def add_gain(which, p):
         total = r.gain_sum[which]
@@ -509,6 +559,7 @@
         return c
 
     row_loop(64, second_back)
+    waves[0].tick()
     r.acc[...] = dot_nt(r.wo[...], r.gb[...])
 
     def gates(h):
@@ -528,26 +579,14 @@
     exchange = Exchange(r, 1, pack, seq)
     exchange.begin()
 
-    jobs = [Job(r, where, k, 4 * k, k * 1024, 0, 512) for k in range(5)]
-
     def block(row, value):
         r.g[row:row + 512, :] = value
 
-    for k in range(2):
-        for j in range(2 * k, 2 * k + 2):
-            block(ROW_DOWN + j * 512, dot_tn(r.xb[j], r.cot[...]))
-        jobs[k].tick()
     r.hidT[...] = r.hid[...].T
-    for k in range(2):
-        for j in range(2 * k, 2 * k + 2):
-            block(ROW_UP + j * 512, dot(r.hidT[...], r.gup[j]))
-        jobs[2 + k].tick()
-    for job in jobs[0:2]:
-        job.tick()
+    for j in range(4):
+        block(ROW_UP + j * 512, dot(r.hidT[...], r.gup[j]))
     block(ROW_O, dot(r.attT[...], r.gb[...]))
-    for job in jobs[2:4]:
-        job.tick()
-    exchange.turn()
+    waves[1].tick()
 
     def map_back(h, gphi, phi, flat, which):
         p = (gphi.astype(BF16).astype(F32) * phi.astype(F32)).astype(BF16)
@@ -558,20 +597,15 @@
     def query_back(h):
         gphi = dot(same(dot_tn(r.gext[h], r.vext[h])), r.phik[h]) + dot_tn(grad_ends(h), r.sb1[h])
         map_back(h, gphi, r.phiq[h], r.qT, 0)
-        r.gvT[h] = dot(r.gext[h, 0:64], same(dot_nt(r.phiq[h], r.phik[h])))
-
-    head_loop(query_back)
+        r.acc2[pl.ds(pl.multiple_of(h * 64, 64), 64)] = dot(r.gext[h, 0:64], same(dot_nt(r.phiq[h], r.phik[h])))
+
+    head_loop(query_back, 0, 3)
+    waves[1].tick()
+    head_loop(query_back, 3, 6)
+    waves[0].tick()
+    exchange.turn()
+    head_loop(query_back, 6, 8)
     block(ROW_Q, dot_nt(r.nT[...], r.gT[0]))
-    jobs[4].tick()
-    for job in jobs[0:4]:
-        job.tick()
-    stores = []
-
-    def store(src, dst):
-        copy = pltpu.make_async_copy(src, dst, r.store.at[len(stores)])
-        copy.start()
-        stores.append(copy)
-
     r.acc[...] = dot(r.xb[0], r.wdown[0])
     for j in range(1, 4):
         r.acc[...] += dot(r.xb[j], r.wdown[j])
@@ -581,9 +615,7 @@
         return c
 
     row_loop(64, put_out)
-    store(r.obf, out_h)
-    for job in jobs:
-        job.tick()
+    waves[0].tick()
     exchange.wait()
 
     def key_back(h):
@@ -592,14 +624,17 @@
         map_back(h, gphi, r.phik[h], r.kT, 1)
         far = dot_nt(r.sb2[h, 0:128], r.phik[h])
         rows = pl.ds(pl.multiple_of(h * 64, 64), 64)
-        r.gT[2, rows] = (r.gvT[h] + jnp.where(in_f, far[0:64], 0.0) + jnp.where(in_l, far[64:128], 0.0)).astype(BF16)
-
-    head_loop(key_back)
+        r.gT[2, rows] = (r.acc2[rows] + jnp.where(in_f, far[0:64], 0.0) + jnp.where(in_l, far[64:128], 0.0)).astype(BF16)
+
+    head_loop(key_back, 0, 4)
+    waves[0].tick()
+    waves[1].tick()
+    head_loop(key_back, 4, 8)
     block(ROW_K, dot_nt(r.nT[...], r.gT[1]))
     block(ROW_V, dot_nt(r.nT[...], r.gT[2]))
-    last = [Job(r, where, k + 1, 20 + k, 5120, k * 128, 128) for k in range(4)]
-    for job in last + jobs:
-        job.tick()
+    waves[2].tick()
+    waves[0].tick()
+    waves[1].tick()
     r.acc2[...] = dot(r.wqkv[0], r.gT[0])
 
     def normed_back(i, c):
@@ -608,8 +643,7 @@
 
     lax.fori_loop(1, 3, normed_back, 0)
     r.acc[...] = r.acc2[...].T
-    for job in last + jobs:
-        job.tick()
+    waves[2].tick()
 
     def first_back(rows, c):
         gn = r.acc[rows, :].astype(BF16).astype(F32)
@@ -619,7 +653,6 @@
         return c
 
     row_loop(64, first_back)
-    store(r.gibf, gin_h)
     for which in range(2):
         total = r.gain_sum[which, 0:1]
         for i in range(1, 8):
@@ -628,41 +661,53 @@
             r.gain_here[4 * which + j:4 * which + j + 1] = total[:, j * 128:(j + 1) * 128]
     gains = Gains(r, pack, seq)
     gains.begin()
-    for job in last + jobs:
-        job.tick()
+    order = (waves[1], waves[2], waves[0])
+    for wave in order:
+        wave.tick()
     gains.turn()
-    while last[0].step < 13 or jobs[4].step < 13:
-        for job in last + jobs:
-            if job.step < 13:
-                job.tick()
+    while not all(wave.done for wave in waves):
+        for wave in order:
+            wave.tick()
     gain_ref[...] = gains.end()
-    for job in jobs + last:
-        job.now.wait()
-    for j in range(4):
-        store(r.g.at[pl.ds(ROW_DOWN + j * 512, 512)], gwdown_h.at[pl.ds(j * 512, 512)])
-        store(r.g.at[pl.ds(ROW_UP + j * 512, 512)], gwup_h.at[:, pl.ds(j * 512, 512)])
-    for row, dst in ((ROW_O, gwo_h), (ROW_Q, gwq_h), (ROW_K, gwk_h), (ROW_V, gwv_h)):
-        store(r.g.at[pl.ds(row, 512)], dst)
-    for copy in stores:
+
+
+def store_kernel(out, gin, g, gain, out_h, gin_h, gwq_h, gwk_h, gwv_h, gwo_h, gwup_h, gwdown_h, gain_h, sems):
+    pieces = [(g.at[pl.ds(ROW_DOWN, FF)], gwdown_h)]
+    pieces += [(g.at[pl.ds(ROW_UP + j * 512, 512)], gwup_h.at[:, pl.ds(j * 512, 512)]) for j in range(4)]
+    pieces += [(g.at[pl.ds(row, 512)], dst) for row, dst in ((ROW_O, gwo_h), (ROW_Q, gwq_h), (ROW_K, gwk_h), (ROW_V, gwv_h))]
+    pieces += [(out, out_h), (gin, gin_h), (gain, gain_h)]
+    copies = [pltpu.make_async_copy(src, dst, sems.at[i]) for i, (src, dst) in enumerate(pieces)]
+    for copy in copies:
+        copy.start()
+    for copy in copies:
         copy.wait()
 
 
 def per_device(
     inputs, w_query, w_key, w_value, w_output, w_up, w_down, gain_attn, gain_ffn, random_features, doc_ids, live_rows, cotangent):
-    any_space = pl.BlockSpec(memory_space=pl.ANY)
+    hbm = pl.BlockSpec(memory_space=pltpu.HBM)
     vmem = pl.BlockSpec(memory_space=pltpu.VMEM)
     f32 = lambda *shape: jax.ShapeDtypeStruct(shape, F32)
     low = jax.ShapeDtypeStruct((T, D), BF16)
+    held = pl.pallas_call(
+        kernel,
+        out_shape=(pltpu.VMEM((T, D), BF16), pltpu.VMEM((T, D), BF16), pltpu.VMEM((6144, 512), F32), pltpu.VMEM((8, 128), F32)),
+        in_specs=[hbm] * 9 + [vmem] * 4,
+        out_specs=(vmem,) * 4,
+        scratch_shapes=[pltpu.VMEM(shape, dtype) for _, shape, dtype in SCRATCH] + [sem for _, sem in SEMS],
+        compiler_params=pltpu.CompilerParams(collective_id=0, has_side_effects=True, vmem_limit_bytes=VMEM_LIMIT),
+    )(
+        *[pltpu.with_memory_space_constraint(v, pltpu.HBM) for v in (
+            inputs[0], w_query, w_key, w_value, w_output, w_up, w_down, random_features, cotangent[0])],
+        gain_attn[None], gain_ffn[None], doc_ids, live_rows)
     outs = pl.pallas_call(
-        kernel,
+        store_kernel,
         out_shape=(low, low, f32(D, D), f32(D, D), f32(D, D), f32(D, D), f32(D, FF), f32(FF, D), f32(8, 128)),
-        in_specs=[any_space] * 9 + [vmem] * 4,
-        out_specs=(any_space,) * 8 + (vmem,),
-        scratch_shapes=[pltpu.VMEM(shape, dtype) for _, shape, dtype in SCRATCH] + [sem for _, sem in SEMS],
-        compiler_params=pltpu.CompilerParams(collective_id=0, has_side_effects=True, vmem_limit_bytes=63 * 2**20),
-    )(
-        inputs[0], w_query, w_key, w_value, w_output, w_up, w_down, random_features, cotangent[0],
-        gain_attn[None], gain_ffn[None], doc_ids, live_rows)
+        in_specs=[vmem] * 4,
+        out_specs=(hbm,) * 9,
+        scratch_shapes=[pltpu.SemaphoreType.DMA((12,))],
+        compiler_params=pltpu.CompilerParams(vmem_limit_bytes=1 * 2**20),
+    )(*held)
     gain = outs[8].reshape(2 * D)
     return (outs[0][None], outs[1][None]) + tuple(outs[2:8]) + (gain[:D], gain[D:])
 

time: 228 us -> 186 us (0.82)
  Pallas kernels: 211 us -> 184 us
  local copies, waits for them, and re-layouts: 16.3 us -> 0.59 us
    pallas_call x1 -> x2, Pallas kernels: 211 us -> 184 us  [the longest x1 179 us: per_device(): pl.pallas_call(kernel, out_shape=(pltpu.VMEM((T, D), BF16), pltpu.VMEM((T...]
    unnamed x18 -> x0, local copies, waits for them, and re-layouts: 14.9 us -> none
where the time goes in v3:
time: 186 us; the launch traced here: 185 us
  Pallas kernels  184 us (99%)
    pallas_call x1, Pallas kernels, per_device(): pl.pallas_call(kernel, out_shape=(pltpu.VMEM((T, D), BF16), pltpu.VMEM((T...  179 us
    pallas_call x1, Pallas kernels, per_device(): pl.pallas_call(store_kernel, out_shape=(low, low, f32(D, D), f32(D, D), f...  4.97 us

profile of v3, /device:TPU:1, one launch (start us, length us, event | category | flops | bytes accessed | tf_op | source)
XLA Modules:
  0.0 185.4 jit_solution(16886574947713707285)
XLA Ops:
  0.6 179.2 %shard_map.204 = (bf16[512,512]{1,0:T(8,128)(2,1)S(1)}, bf16[512,512]{1,0:T(8,128)(2,1)S(1)}, f32[6144,512]{1,0:T(8,128)S(1)}, f32[8,128]{1,0:T(8,128)S(1)}) custom-call(bf16[512,512]{1,0:T(8,128)(2,1)} %bitcast.10, bf16[512,512]{1,0:T(8,128)(2,1)} %wq_h.1, bf16[512,512]{1,0:T(8,128)(2,1)} %wk_h.1, bf16[512,512]{1,0:T(8,128)(2,1)} %wv_h.1, ...), custom_call_target="tpu_custom_call" | custom-call | tf_op jit(solution)/shard_map/pallas_call | solution.py:692
  179.9 5.0 %shard_map.205 = (bf16[512,512]{1,0:T(8,128)(2,1)}, bf16[512,512]{1,0:T(8,128)(2,1)}, f32[512,512]{1,0:T(8,128)}, f32[512,512]{1,0:T(8,128)}, f32[512,512]{1,0:T...) custom-call(bf16[512,512]{1,0:T(8,128)(2,1)S(1)} %get-tuple-element.23.out, ...), custom_call_target="tpu_custom_call" | custom-call | tf_op jit(solution)/shard_map/pallas_call | solution.py:703
  184.8 0.6 slice_bitcast_fusion

commit v4 on v3

--- a/solution.py
+++ b/solution.py
@@ -13,7 +13,7 @@
 T, D, H, DH, M, FF = 512, 512, 8, 64, 256, 2048
 SLAB = 136
 EPS = 1e-05
-VMEM_LIMIT = 46 * 2**20
+VMEM_LIMIT = 47 * 2**20
 C = DH ** -0.25
 ALPHA = C * math.log2(math.e)
 GELU_A, GELU_B = math.sqrt(2.0 / math.pi), 0.044715
@@ -37,7 +37,7 @@
 
 def place():
     pack, seq = lax.axis_index("pack"), lax.axis_index("seq")
-    return pack // 2, pack % 2, seq // 4, seq % 4
+    return pack >> 1, pack & 1, seq >> 2, seq & 3
 
 
 def layer_norm(v):
@@ -65,136 +65,154 @@
     lax.fori_loop(start, stop, run, 0)
 
 
-class Wave:
-    def __init__(self, r, where, row, parts, first):
-        self.parts = []
-        for k, rows in enumerate(parts):
-            self.parts.append(Part(r, where, row, rows // 2, k, first + k))
-            row += rows
-        self.done = False
-
-    def tick(self):
-        if self.done:
-            return
-        for part in self.parts:
-            part.finish()
-            part.start()
-        self.done = self.parts[0].step == 8
+def wait_all(like, send_sem, recv_sem, dev):
+    pltpu.make_async_remote_copy(
+        src_ref=like, dst_ref=like, send_sem=send_sem, recv_sem=recv_sem, device_id=dev, device_id_type=MESH).wait()
 
 
 class Part:
-    def __init__(self, r, where, row, n, color, sem):
-        self.r, self.where, self.row, self.n, self.sem = r, where, row, n, sem
-        self.axes = [(color + i) % 3 for i in range(3)]
-        self.at = row + where[1] * n
+    def __init__(self, r, where, number, row, rows, axes, down, up):
+        self.r, self.where, self.row, self.n = r, where, row, rows // 2
+        self.axes = dict(zip("oic", axes))
+        self.down, self.up = down, up
+        self.number = number
+        self.at = row + where[1] * self.n
         self.buf = row // 2
-        self.step = -1
-        self.copies = []
-
-    def peers(self, stage):
+        self.step, self.last = -1, len(down) + len(up) + 1
+        self.flying, self.held, self.freed = 0, {}, set()
+
+    def mine(self, role):
         z, core, x, y = self.where
-        axis = self.axes[stage]
-        mine = (x, y, z)[axis]
-        devs = []
-        for d in range(1, 4):
-            there = (mine + d) % 4
-            x2, y2, z2 = (there if axis == 0 else x), (there if axis == 1 else y), (there if axis == 2 else z)
-            devs.append((there, (z2 * 2 + core, x2 * 4 + y2)))
-        return mine, devs
+        return (x, y, z)[self.axes[role]]
+
+    def peers(self, roles):
+        z, core, x, y = self.where
+        out = []
+        for far in range(1, 4 ** len(roles)):
+            at = {role: (self.mine(role) + far // 4 ** k) & 3 for k, role in enumerate(roles)}
+            spot = [x, y, z]
+            for role, there in at.items():
+                spot[self.axes[role]] = there
+            out.append((at, (spot[2] * 2 + core, spot[0] * 4 + spot[1])))
+        return out
+
+    def behind(self, roles, d):
+        return {role: (self.mine(role) - (d + 1) // 4 ** k) & 3 for k, role in enumerate(roles)}
 
     def sibling(self):
         z, core, x, y = self.where
         return (z * 2 + 1 - core, x * 4 + y)
 
-    def rows(self, at, count):
-        return pl.ds(pl.multiple_of(at, 8), count)
-
-    def lanes(self, quarter):
-        return pl.ds(pl.multiple_of(quarter * 128, 128), 128)
-
-    def send(self, src, dst, dev, d):
-        copy = pltpu.make_async_remote_copy(
-            src_ref=src, dst_ref=dst, send_sem=self.r.ssem.at[self.sem, self.step, d], recv_sem=self.r.rsem.at[self.sem, self.step, d],
-            device_id=dev, device_id_type=MESH)
-        copy.start()
-        self.copies.append(copy)
-
-    def free(self, stage):
-        for _, dev in self.peers(stage)[1]:
-            pl.semaphore_signal(self.r.free.at[self.sem, stage], inc=1, device_id=dev, device_id_type=MESH)
-
-    def add(self, count, buf, slots):
-        r, step = self.r, min(32, count)
+    def block(self, at={}):
+        at = {**self.held, **at}
+        row, rows, lane, lanes = self.at, self.n, 0, 512
+        if "o" in at:
+            row, rows = row + at["o"] * (self.n // 4), self.n // 4
+        if "i" in at:
+            row, rows = row + at["i"] * (self.n // 16), self.n // 16
+        if "c" in at:
+            lane, lanes = pl.multiple_of(at["c"] * 128, 128), 128
+        return row, rows, lane, lanes
+
+    def view(self, block):
+        row, rows, lane, lanes = block
+        return self.r.g.at[pl.ds(pl.multiple_of(row, 8), rows), pl.ds(lane, lanes)]
+
+    def landing(self, roles, d):
+        n = self.n
+        row, lane = {
+            "o": (d * (n // 4), 0),
+            "ic": (3 * n // 4 + d // 4 * (n // 16), d % 4 * 128),
+            "c": (0, d * 128),
+            "oi": (d * (n // 16), 384),
+        }[roles]
+        return self.buf + row, lane
+
+    def send(self, src, dst, dev):
+        pltpu.make_async_remote_copy(
+            src_ref=src, dst_ref=dst, send_sem=self.r.ssem.at[self.number], recv_sem=self.r.rsem.at[self.number, self.step],
+            device_id=dev, device_id_type=MESH).start()
+        self.flying += 1
+        self.piece = src.shape
+
+    def add(self, block, buf, slots):
+        r = self.r
+        row, rows, lane, lanes = block
+        step = min(16384 // lanes, rows)
 
         def body(i, c):
-            at = self.rows(self.at + i * step, step)
-            total = r.g[at, :]
-            for slot in slots:
-                total = total + buf[self.rows(slot + i * step, step), :]
-            r.g[at, :] = total
+            at = pl.ds(pl.multiple_of(row + i * step, 8), step)
+            total = r.g[at, pl.ds(lane, lanes)]
+            for slot, column in slots:
+                total = total + buf[pl.ds(pl.multiple_of(slot + i * step, 8), step), pl.ds(column, lanes)]
+            r.g[at, pl.ds(lane, lanes)] = total
             return c
 
-        lax.fori_loop(0, count // step, body, 0)
+        lax.fori_loop(0, rows // step, body, 0)
 
     def finish(self):
-        r, n, s = self.r, self.n, self.step
-        for copy in self.copies:
-            copy.wait()
-        self.copies = []
+        r, s, downs = self.r, self.step, len(self.down)
+        if self.flying:
+            rows, lanes = self.piece
+            wait_all(r.from_chip.at[pl.ds(0, self.flying * rows), pl.ds(0, lanes)], r.ssem.at[self.number], r.rsem.at[self.number, s], self.sibling())
+        self.flying = 0
         if s == 0:
-            pl.semaphore_signal(r.free.at[self.sem, 2], inc=1, device_id=self.sibling(), device_id_type=MESH)
-            self.add(n, r.from_core, [self.buf])
-        elif s in (1, 2):
-            q = n // 4 ** s
-            base = self.buf + (0 if s == 1 else 3 * n // 4)
-            self.free(s - 1)
-            self.at = self.at + self.peers(s - 1)[0] * q
-            self.add(q, r.from_chip, [base + d * q for d in range(3)])
-        elif s == 3:
-            q = n // 16
-            at, mine = self.rows(self.at, q), self.lanes(self.peers(2)[0])
-            buf = pl.ds(self.buf + 15 * n // 16, q)
-            r.g[at, mine] = r.g[at, mine] + r.from_chip[buf, 0:128] + r.from_chip[buf, 128:256] + r.from_chip[buf, 256:384]
-        elif s == 4:
-            q = n // 16
-            at, mine = self.rows(self.at, q), self.peers(2)[0]
-            for d in range(3):
-                r.g[at, self.lanes((mine + 3 - d) % 4)] = r.turn[d, self.buf // 16:self.buf // 16 + q]
-        elif s in (5, 6):
-            q = n // 4 ** (7 - s)
-            self.at = self.at - self.peers(6 - s)[0] * q
+            pl.semaphore_signal(r.free.at[self.number, 0], inc=1, device_id=self.sibling(), device_id_type=MESH)
+            self.add(self.block(), r.from_core, [(self.buf, 0)])
+        elif 1 <= s <= downs:
+            roles = self.down[s - 1]
+            self.held.update({role: self.mine(role) for role in roles})
+            for k in range(1, len(self.up)):
+                if k not in self.freed and set(self.up[k]) <= set(self.held):
+                    self.freed.add(k)
+                    for _, dev in self.peers(self.up[k]):
+                        pl.semaphore_signal(r.free.at[self.number, k], inc=1, device_id=dev, device_id_type=MESH)
+            self.add(self.block(), r.from_chip, [self.landing(roles, d) for d in range(4 ** len(roles) - 1)])
+        elif downs < s < self.last:
+            roles = self.up[s - downs - 1]
+            if s == downs + 1:
+                for d in range(4 ** len(roles) - 1):
+                    row, rows, lane, lanes = self.block(self.behind(roles, d))
+                    r.g[pl.ds(pl.multiple_of(row, 8), rows), pl.ds(lane, lanes)] = r.turn[d, pl.ds(self.buf // 16, rows)]
+            for role in roles:
+                del self.held[role]
 
     def start(self):
-        r, n = self.r, self.n
+        r, n, downs = self.r, self.n, len(self.down)
         self.step = s = self.step + 1
         if s == 0:
             core = self.where[1]
-            self.send(r.g.at[self.rows(self.row + (1 - core) * n, n)], r.from_core.at[pl.ds(self.buf, n)], self.sibling(), 0)
-        elif s in (1, 2):
-            q = n // 4 ** s
-            base = self.buf + (0 if s == 1 else 3 * n // 4)
-            for d, (there, dev) in enumerate(self.peers(s - 1)[1]):
-                self.send(r.g.at[self.rows(self.at + there * q, q)], r.from_chip.at[pl.ds(base + d * q, q)], dev, d)
-        elif s == 3:
-            q = n // 16
-            at = self.rows(self.at, q)
-            for d, (there, dev) in enumerate(self.peers(2)[1]):
-                self.send(r.g.at[at, self.lanes(there)], r.from_chip.at[pl.ds(self.buf + 15 * n // 16, q), pl.ds(d * 128, 128)], dev, d)
-        elif s == 4:
-            q = n // 16
-            mine, devs = self.peers(2)
-            for d, (there, dev) in enumerate(devs):
-                self.send(r.g.at[self.rows(self.at, q), self.lanes(mine)], r.turn.at[d, pl.ds(self.buf // 16, q)], dev, d)
-        elif s in (5, 6):
-            q = n // 4 ** (7 - s)
-            part = r.g.at[self.rows(self.at, q)]
-            pl.semaphore_wait(r.free.at[self.sem, 6 - s], 3)
-            for d, (there, dev) in enumerate(self.peers(6 - s)[1]):
-                self.send(part, part, dev, d)
-        elif s == 7:
-            part = r.g.at[self.rows(self.at, n)]
-            pl.semaphore_wait(r.free.at[self.sem, 2], 1)
-            self.send(part, part, self.sibling(), 0)
+            self.send(r.g.at[pl.ds(pl.multiple_of(self.row + (1 - core) * n, 8), n)], r.from_core.at[pl.ds(self.buf, n)], self.sibling())
+        elif 1 <= s <= downs:
+            roles = self.down[s - 1]
+            for d, (at, dev) in enumerate(self.peers(roles)):
+                block = self.block(at)
+                row, lane = self.landing(roles, d)
+                self.send(self.view(block), r.from_chip.at[pl.ds(row, block[1]), pl.ds(lane, block[3])], dev)
+        elif downs < s < self.last:
+            k = s - downs - 1
+            roles = self.up[k]
+            block = self.block()
+            part = self.view(block)
+            peers = self.peers(roles)
+            if k > 0:
+                pl.semaphore_wait(r.free.at[self.number, k], len(peers))
+            for d, (at, dev) in enumerate(peers):
+                self.send(part, part if k > 0 else r.turn.at[d, pl.ds(self.buf // 16, block[1])], dev)
+        elif s == self.last:
+            part = self.view(self.block())
+            pl.semaphore_wait(r.free.at[self.number, 0], 1)
+            self.send(part, part, self.sibling())
+
+    def tick(self):
+        if self.step <= self.last:
+            self.finish()
+            self.start()
+
+
+def tick(*parts):
+    for part in parts:
+        part.tick()
 
 
 class Exchange:
@@ -202,27 +220,23 @@
         self.r, self.sems, self.pack, self.seq = r, r.esem.at[which], pack, seq
 
     def send(self, src, dst, way):
-        copies = []
         for step in range(1, 16):
-            peer = lax.rem(self.seq + step, 16)
-            copy = pltpu.make_async_remote_copy(
-                src_ref=src.at[peer], dst_ref=dst.at[self.seq],
-                send_sem=self.sems.at[2 * way, step - 1], recv_sem=self.sems.at[2 * way + 1, step - 1],
-                device_id=(self.pack, peer), device_id_type=MESH)
-            copy.start()
-            copies.append(copy)
+            peer = (self.seq + step) & 15
+            pltpu.make_async_remote_copy(
+                src_ref=src.at[peer], dst_ref=dst.at[self.seq], send_sem=self.sems.at[2], recv_sem=self.sems.at[way],
+                device_id=(self.pack, peer), device_id_type=MESH).start()
         dst[self.seq] = src[self.seq]
-        self.copies = copies
+        self.way = way
 
     def wait(self):
-        for copy in self.copies:
-            copy.wait()
+        wait_all(self.r.arrived.at[pl.ds(0, 15)], self.sems.at[2], self.sems.at[self.way], (self.pack, (self.seq + 1) & 15))
 
     def begin(self):
         self.send(self.r.out, self.r.arrived, 0)
 
-    def turn(self):
+    def turn(self, between=lambda: None):
         self.wait()
+        between()
         arrived, back = self.r.arrived, self.r.back
 
         def left(dev, carry):
@@ -263,21 +277,20 @@
         self.r, self.pack, self.seq = r, pack, seq
 
     def send(self, src, dst, way, size):
-        self.copies = []
         for step in range(1, size):
-            dev = (lax.rem(self.pack + step, 8), self.seq) if way == 0 else (self.pack, lax.rem(self.seq + step, 16))
-            copy = pltpu.make_async_remote_copy(
-                src_ref=src, dst_ref=dst.at[step - 1], send_sem=self.r.gsem.at[2 * way, step - 1],
-                recv_sem=self.r.gsem.at[2 * way + 1, step - 1], device_id=dev, device_id_type=MESH)
-            copy.start()
-            self.copies.append(copy)
+            dev = ((self.pack + step) & 7, self.seq) if way == 0 else (self.pack, (self.seq + step) & 15)
+            pltpu.make_async_remote_copy(
+                src_ref=src, dst_ref=dst.at[step - 1], send_sem=self.r.gsem.at[2], recv_sem=self.r.gsem.at[way],
+                device_id=dev, device_id_type=MESH).start()
+
+    def wait(self, like, way):
+        wait_all(like, self.r.gsem.at[2], self.r.gsem.at[way], (self.pack, (self.seq + 1) & 15))
 
     def begin(self):
         self.send(self.r.gain_here, self.r.gain_pack, 0, 8)
 
     def turn(self):
-        for copy in self.copies:
-            copy.wait()
+        self.wait(self.r.gain_pack, 0)
         total = self.r.gain_here[...]
         for i in range(7):
             total = total + self.r.gain_pack[i]
@@ -285,8 +298,7 @@
         self.send(self.r.gain_mid, self.r.gain_seq, 1, 16)
 
     def end(self):
-        for copy in self.copies:
-            copy.wait()
+        self.wait(self.r.gain_seq, 1)
         total = self.r.gain_mid[...]
         for i in range(15):
             total = total + self.r.gain_seq[i]
@@ -313,14 +325,12 @@
     ("acc", (T, D), F32), ("acc2", (T, D), F32), ("gmid", (T, D), F32),
     ("sb1", (H, 144, M), BF16), ("sb2", (H, 144, M), BF16),
             ("out", (16, SLAB, 128), F32), ("arrived", (16, SLAB, 128), F32), ("got", (16, SLAB, 128), F32),
-    ("from_core", (3072, 512), F32), ("from_chip", (3072, 512), F32), ("turn", (3, 192, 128), F32),
+    ("from_core", (3072, 512), F32), ("from_chip", (3072, 512), F32), ("turn", (15, 192, 128), F32),
     ("gain_sum", (2, 8, D), F32), ("gain_here", (8, 128), F32), ("gain_pack", (7, 8, 128), F32), ("gain_mid", (8, 128), F32), ("gain_seq", (15, 8, 128), F32),
 ]
 SEMS = [
-    ("load", pltpu.SemaphoreType.DMA((20,))),
-    ("esem", pltpu.SemaphoreType.DMA((2, 4, 15))), ("gsem", pltpu.SemaphoreType.DMA((4, 15))),
-    ("ssem", pltpu.SemaphoreType.DMA((9, 8, 3))), ("rsem", pltpu.SemaphoreType.DMA((9, 8, 3))),
-    ("free", pltpu.SemaphoreType.REGULAR((9, 3))),
+    ("load", pltpu.SemaphoreType.DMA((9,))), ("esem", pltpu.SemaphoreType.DMA((2, 3))), ("gsem", pltpu.SemaphoreType.DMA((3,))),
+    ("ssem", pltpu.SemaphoreType.DMA((11,))), ("rsem", pltpu.SemaphoreType.DMA((11, 6))), ("free", pltpu.SemaphoreType.REGULAR((11, 2))),
 ]
 ROW_DOWN, ROW_UP, ROW_O, ROW_Q, ROW_K, ROW_V = 0, 2048, 4096, 4608, 5120, 5632
 
@@ -346,20 +356,14 @@
 
     load("x", x_h, r.x)
     load("wk", wk_h, r.wqkv.at[1])
+    load("rf", rf_h, r.rf)
     load("wv", wv_h, r.wqkv.at[2])
-    load("rf", rf_h, r.rf)
     load("wq", wq_h, r.wqkv.at[0])
-    load("wo", wo_h, r.wo)
-    for j in range(4):
-        load("wup%d" % j, wup_h.at[:, pl.ds(j * 512, 512)], r.wup.at[j])
-    load("cot", cot_h, r.cot)
-    for j in range(4):
-        load("wdown%d" % j, wdown_h.at[pl.ds(j * 512, 512)], r.wdown.at[j])
     barrier = pltpu.get_barrier_semaphore()
     for step in range(1, 16):
-        pl.semaphore_signal(barrier, inc=1, device_id=(pack, lax.rem(seq + step, 16)), device_id_type=MESH)
+        pl.semaphore_signal(barrier, inc=1, device_id=(pack, (seq + step) & 15), device_id_type=MESH)
     for step in range(1, 8):
-        pl.semaphore_signal(barrier, inc=1, device_id=(lax.rem(pack + step, 8), seq), device_id_type=MESH)
+        pl.semaphore_signal(barrier, inc=1, device_id=((pack + step) & 7, seq), device_id_type=MESH)
 
     doc = doc_ref[...].astype(F32)
     doc_f, doc_l = doc[:, 0:1], doc[:, T - 1:T]
@@ -457,6 +461,11 @@
     pl.semaphore_wait(barrier, 22)
     exchange = Exchange(r, 0, pack, seq)
     exchange.begin()
+    load("wo", wo_h, r.wo)
+    load("cot", cot_h, r.cot)
+    for j in range(4):
+        pltpu.make_async_copy(wup_h.at[:, pl.ds(j * 512, 512)], r.wup.at[j], r.load.at[7]).start()
+        pltpu.make_async_copy(wdown_h.at[pl.ds(j * 512, 512)], r.wdown.at[j], r.load.at[8]).start()
 
     r.nT[...] = r.nb[...].T
     loads["wq"].wait()
@@ -500,9 +509,8 @@
     row_loop(64, second_norm)
 
     loads["cot"].wait()
-    for j in range(4):
-        loads["wup%d" % j].wait()
-        loads["wdown%d" % j].wait()
+    pltpu.make_async_copy(r.wup, r.wup, r.load.at[7]).wait()
+    pltpu.make_async_copy(r.wdown, r.wdown, r.load.at[8]).wait()
 
     def feed(j, c):
         r.acc[...] = dot(r.hid[...], r.wup[j])
@@ -522,24 +530,30 @@
         row_loop(16, gelu)
         back = dot_nt(r.gup[j], r.wup[j])
 
-        @pl.when(j == 0)
-        def _():
-            r.gmid[...] = back
-
-        @pl.when(j > 0)
-        def _():
-            r.gmid[...] += back
-
-        r.g[pl.ds(pl.multiple_of(ROW_DOWN + j * 512, 512), 512), :] = dot_tn(r.xb[j], r.cot[...])
+        r.gmid[...] = back if j == 0 else r.gmid[...] + back
+        r.g[ROW_DOWN + j * 512:ROW_DOWN + (j + 1) * 512, :] = dot_tn(r.xb[j], r.cot[...])
         return c
 
-    lax.fori_loop(0, 4, feed, 0)
-    waves = [
-        Wave(r, where, ROW_DOWN, (512, 768, 768), 0),
-        Wave(r, where, ROW_UP, (768, 768, 1024), 3),
-        Wave(r, where, ROW_Q, (512, 512, 512), 6),
+    X, Y, Z = 0, 1, 2
+    early = [
+        Part(r, where, k, ROW_DOWN + 512 * k, 512, axes, ("o", "ic"), ("ic", "o"))
+        for k, axes in enumerate(((X, Y, Z), (Y, Z, X), (Z, X, Y), (Z, Y, X)))
     ]
-    waves[0].tick()
+    up = [
+        Part(r, where, 4, ROW_UP, 1024, (X, Y, Z), ("c", "oi"), ("oi", "c")),
+        Part(r, where, 5, ROW_UP + 1024, 512, (X, Y, Z), ("c", "oi"), ("ic", "o")),
+        Part(r, where, 6, ROW_UP + 1536, 512, (Y, X, Z), ("c", "oi"), ("ic", "o")),
+    ]
+    branch = Part(r, where, 7, ROW_O, 512, (Z, X, Y), ("o", "ic"), ("ic", "o"))
+    last = [
+        Part(r, where, 8, ROW_Q, 512, (X, Y, Z), ("o", "ic"), ("ic", "o")),
+        Part(r, where, 9, ROW_Q + 512, 512, (Y, Z, X), ("o", "ic"), ("ic", "o")),
+        Part(r, where, 10, ROW_Q + 1024, 512, (Z, X, Y), ("o", "ic"), ("ic", "o")),
+    ]
+
+    for j in range(4):
+        feed(j, 0)
+        tick(*early[max(j - 1, 0):j + 1])
 
     def add_gain(which, p):
         total = r.gain_sum[which]
@@ -559,7 +573,7 @@
         return c
 
     row_loop(64, second_back)
-    waves[0].tick()
+    tick(early[3])
     r.acc[...] = dot_nt(r.wo[...], r.gb[...])
 
     def gates(h):
@@ -586,7 +600,7 @@
     for j in range(4):
         block(ROW_UP + j * 512, dot(r.hidT[...], r.gup[j]))
     block(ROW_O, dot(r.attT[...], r.gb[...]))
-    waves[1].tick()
+    tick(*up, branch)
 
     def map_back(h, gphi, phi, flat, which):
         p = (gphi.astype(BF16).astype(F32) * phi.astype(F32)).astype(BF16)
@@ -600,11 +614,10 @@
         r.acc2[pl.ds(pl.multiple_of(h * 64, 64), 64)] = dot(r.gext[h, 0:64], same(dot_nt(r.phiq[h], r.phik[h])))
 
     head_loop(query_back, 0, 3)
-    waves[1].tick()
-    head_loop(query_back, 3, 6)
-    waves[0].tick()
+    tick(*up, branch)
+    head_loop(query_back, 3, 8)
     exchange.turn()
-    head_loop(query_back, 6, 8)
+    tick(*early)
     block(ROW_Q, dot_nt(r.nT[...], r.gT[0]))
     r.acc[...] = dot(r.xb[0], r.wdown[0])
     for j in range(1, 4):
@@ -615,26 +628,29 @@
         return c
 
     row_loop(64, put_out)
-    waves[0].tick()
+
+    def key_local(h):
+        gphi = dot(same(dot_tn(r.vext[h], r.gext[h])), r.phiq[h]).astype(BF16)
+        r.xb[h // 2, :, pl.ds(pl.multiple_of(h % 2 * 256, 256), 256)] = gphi
+
+    head_loop(key_local)
     exchange.wait()
+    tick(*early)
 
     def key_back(h):
         take_slab(h, r.sb2)
-        gphi = dot(same(dot_tn(r.vext[h], r.gext[h])), r.phiq[h]) + dot_tn(value_ends(h), r.sb2[h])
+        gphi = r.xb[h // 2, :, pl.ds(pl.multiple_of(h % 2 * 256, 256), 256)].astype(F32) + dot_tn(value_ends(h), r.sb2[h])
         map_back(h, gphi, r.phik[h], r.kT, 1)
         far = dot_nt(r.sb2[h, 0:128], r.phik[h])
         rows = pl.ds(pl.multiple_of(h * 64, 64), 64)
         r.gT[2, rows] = (r.acc2[rows] + jnp.where(in_f, far[0:64], 0.0) + jnp.where(in_l, far[64:128], 0.0)).astype(BF16)
 
     head_loop(key_back, 0, 4)
-    waves[0].tick()
-    waves[1].tick()
+    tick(*up)
     head_loop(key_back, 4, 8)
     block(ROW_K, dot_nt(r.nT[...], r.gT[1]))
     block(ROW_V, dot_nt(r.nT[...], r.gT[2]))
-    waves[2].tick()
-    waves[0].tick()
-    waves[1].tick()
+    tick(*last)
     r.acc2[...] = dot(r.wqkv[0], r.gT[0])
 
     def normed_back(i, c):
@@ -643,7 +659,8 @@
 
     lax.fori_loop(1, 3, normed_back, 0)
     r.acc[...] = r.acc2[...].T
-    waves[2].tick()
+    tick(*last)
+    tick(*early, *up, branch)
 
     def first_back(rows, c):
         gn = r.acc[rows, :].astype(BF16).astype(F32)
@@ -661,21 +678,28 @@
             r.gain_here[4 * which + j:4 * which + j + 1] = total[:, j * 128:(j + 1) * 128]
     gains = Gains(r, pack, seq)
     gains.begin()
-    order = (waves[1], waves[2], waves[0])
-    for wave in order:
-        wave.tick()
+    tick(*last)
+    tick(*up, branch)
+    tick(*last)
+    tick(*early, branch)
     gains.turn()
-    while not all(wave.done for wave in waves):
-        for wave in order:
-            wave.tick()
-    gain_ref[...] = gains.end()
-
-
-def store_kernel(out, gin, g, gain, out_h, gin_h, gwq_h, gwk_h, gwv_h, gwo_h, gwup_h, gwdown_h, gain_h, sems):
+    tick(*last)
+    tick(*up)
+    tick(*last)
+    for part in early + up + [branch] + last:
+        while part.step <= part.last:
+            part.tick()
+    total = gains.end()
+    for j in range(4):
+        gain_ref[0:1, j * 128:(j + 1) * 128] = total[j:j + 1]
+        gain_ref[1:2, j * 128:(j + 1) * 128] = total[4 + j:5 + j]
+
+
+def store_kernel(out, gin, g, gain, out_h, gin_h, gwq_h, gwk_h, gwv_h, gwo_h, gwup_h, gwdown_h, gga_h, ggf_h, sems):
     pieces = [(g.at[pl.ds(ROW_DOWN, FF)], gwdown_h)]
     pieces += [(g.at[pl.ds(ROW_UP + j * 512, 512)], gwup_h.at[:, pl.ds(j * 512, 512)]) for j in range(4)]
     pieces += [(g.at[pl.ds(row, 512)], dst) for row, dst in ((ROW_O, gwo_h), (ROW_Q, gwq_h), (ROW_K, gwk_h), (ROW_V, gwv_h))]
-    pieces += [(out, out_h), (gin, gin_h), (gain, gain_h)]
+    pieces += [(out, out_h), (gin, gin_h), (gain.at[pl.ds(0, 1)], gga_h), (gain.at[pl.ds(1, 1)], ggf_h)]
     copies = [pltpu.make_async_copy(src, dst, sems.at[i]) for i, (src, dst) in enumerate(pieces)]
     for copy in copies:
         copy.start()
@@ -691,7 +715,7 @@
     low = jax.ShapeDtypeStruct((T, D), BF16)
     held = pl.pallas_call(
         kernel,
-        out_shape=(pltpu.VMEM((T, D), BF16), pltpu.VMEM((T, D), BF16), pltpu.VMEM((6144, 512), F32), pltpu.VMEM((8, 128), F32)),
+        out_shape=(pltpu.VMEM((T, D), BF16), pltpu.VMEM((T, D), BF16), pltpu.VMEM((6144, 512), F32), pltpu.VMEM((8, D), F32)),
         in_specs=[hbm] * 9 + [vmem] * 4,
         out_specs=(vmem,) * 4,
         scratch_shapes=[pltpu.VMEM(shape, dtype) for _, shape, dtype in SCRATCH] + [sem for _, sem in SEMS],
@@ -702,14 +726,13 @@
         gain_attn[None], gain_ffn[None], doc_ids, live_rows)
     outs = pl.pallas_call(
         store_kernel,
-        out_shape=(low, low, f32(D, D), f32(D, D), f32(D, D), f32(D, D), f32(D, FF), f32(FF, D), f32(8, 128)),
+        out_shape=(low, low, f32(D, D), f32(D, D), f32(D, D), f32(D, D), f32(D, FF), f32(FF, D), f32(1, D), f32(1, D)),
         in_specs=[vmem] * 4,
-        out_specs=(hbm,) * 9,
-        scratch_shapes=[pltpu.SemaphoreType.DMA((12,))],
+        out_specs=(hbm,) * 10,
+        scratch_shapes=[pltpu.SemaphoreType.DMA((13,))],
         compiler_params=pltpu.CompilerParams(vmem_limit_bytes=1 * 2**20),
     )(*held)
-    gain = outs[8].reshape(2 * D)
-    return (outs[0][None], outs[1][None]) + tuple(outs[2:8]) + (gain[:D], gain[D:])
+    return (outs[0][None], outs[1][None]) + tuple(outs[2:8]) + (outs[8][0], outs[9][0])
 
 
 def solution(mesh):

time: 186 us -> 175 us (0.941)
  Pallas kernels: 184 us -> 173 us
    pallas_call x1, Pallas kernels: 179 us -> 168 us  [per_device(): pl.pallas_call(kernel, out_shape=(pltpu.VMEM((T, D), BF16), pltpu.VMEM((T...]
where the time goes in v4:
time: 175 us; the launch traced here: 174 us
  Pallas kernels  173 us (99%)
    pallas_call x1, Pallas kernels, per_device(): pl.pallas_call(kernel, out_shape=(pltpu.VMEM((T, D), BF16), pltpu.VMEM((T...  168 us
    pallas_call x1, Pallas kernels, per_device(): pl.pallas_call(store_kernel, out_shape=(low, low, f32(D, D), f32(D, D), f...  4.98 us

profile of v4, /device:TPU:1, one launch (start us, length us, event | category | flops | bytes accessed | tf_op | source)
XLA Modules:
  0.0 174.1 jit_solution(13156729761905631)
XLA Ops:
  0.6 168.3 %shard_map.204 = (bf16[512,512]{1,0:T(8,128)(2,1)S(1)}, bf16[512,512]{1,0:T(8,128)(2,1)S(1)}, f32[6144,512]{1,0:T(8,128)S(1)}, f32[8,512]{1,0:T(8,128)S(1)}) custom-call(bf16[512,512]{1,0:T(8,128)(2,1)} %bitcast.8, bf16[512,512]{1,0:T(8,128)(2,1)} %wq_h.1, bf16[512,512]{1,0:T(8,128)(2,1)} %wk_h.1, bf16[512,512]{1,0:T(8,128)(2,1)} %wv_h.1, ...), custom_call_target="tpu_custom_call" | custom-call | tf_op jit(solution)/shard_map/pallas_call | solution.py:716
  169.0 5.0 %shard_map.205 = (bf16[512,512]{1,0:T(8,128)(2,1)}, bf16[512,512]{1,0:T(8,128)(2,1)}, f32[512,512]{1,0:T(8,128)}, f32[512,512]{1,0:T(8,128)}, f32[512,512]{1,0:T...) custom-call(bf16[512,512]{1,0:T(8,128)(2,1)S(1)} %get-tuple-element., ...), custom_call_target="tpu_custom_call" | custom-call | tf_op jit(solution)/shard_map/pallas_call | solution.py:727

commit v5 on v4

--- a/solution.py
+++ b/solution.py
@@ -216,60 +216,74 @@
 
 
 class Exchange:
+    PIECES = (pl.ds(64, SLAB - 64), pl.ds(0, 64))
+
     def __init__(self, r, which, pack, seq):
         self.r, self.sems, self.pack, self.seq = r, r.esem.at[which], pack, seq
 
-    def send(self, src, dst, way):
+    def send(self, src, dst, way, piece):
+        rows = self.PIECES[piece]
         for step in range(1, 16):
             peer = (self.seq + step) & 15
             pltpu.make_async_remote_copy(
-                src_ref=src.at[peer], dst_ref=dst.at[self.seq], send_sem=self.sems.at[2], recv_sem=self.sems.at[way],
-                device_id=(self.pack, peer), device_id_type=MESH).start()
-        dst[self.seq] = src[self.seq]
-        self.way = way
+                src_ref=src.at[peer, rows], dst_ref=dst.at[self.seq, rows], send_sem=self.sems.at[4 + piece],
+                recv_sem=self.sems.at[2 * way + piece], device_id=(self.pack, peer), device_id_type=MESH).start()
+        dst[self.seq, rows] = src[self.seq, rows]
+
+    def wait_piece(self, way, piece):
+        wait_all(
+            self.r.arrived.at[pl.ds(0, 15), self.PIECES[piece]], self.sems.at[4 + piece], self.sems.at[2 * way + piece],
+            (self.pack, (self.seq + 1) & 15))
 
     def wait(self):
-        wait_all(self.r.arrived.at[pl.ds(0, 15)], self.sems.at[2], self.sems.at[self.way], (self.pack, (self.seq + 1) & 15))
+        self.wait_piece(1, 0)
+        self.wait_piece(1, 1)
 
     def begin(self):
-        self.send(self.r.out, self.r.arrived, 0)
-
-    def turn(self, between=lambda: None):
-        self.wait()
-        between()
+        self.send(self.r.out, self.r.arrived, 0, 0)
+        self.send(self.r.out, self.r.arrived, 0, 1)
+
+    def turn(self):
         arrived, back = self.r.arrived, self.r.back
+        none, small_none = jnp.zeros((64, 128), F32), jnp.zeros((1, 128), F32)
 
         def left(dev, carry):
             total, small = carry
             tail, mine = arrived[dev - 1, 128:136], arrived[dev, 128:136]
-            whole = tail[2:3] == tail[3:4]
-            joins = tail[3:4] == mine[2:3]
+            whole, joins = tail[2:3] == tail[3:4], tail[3:4] == mine[2:3]
             total = jnp.where(joins, arrived[dev - 1, 64:128] + jnp.where(whole, total, 0.0), 0.0)
             small = jnp.where(joins, tail[1:2] + jnp.where(whole, small, 0.0), 0.0)
-            back[dev, 0:64] = total
+            back[dev, 64:128] = total
             back[dev, 128:129] = small
             return total, small
 
-        def right(i, carry):
+        def right_small(i, small):
             dev = 14 - i
-            total, small = carry
             tail, mine = arrived[dev + 1, 128:136], arrived[dev, 128:136]
-            whole = tail[2:3] == tail[3:4]
-            joins = mine[3:4] == tail[2:3]
+            whole, joins = tail[2:3] == tail[3:4], mine[3:4] == tail[2:3]
+            small = jnp.where(joins, tail[0:1] + jnp.where(whole, small, 0.0), 0.0)
+            back[dev, 129:130] = small
+            return small
+
+        def right(i, total):
+            dev = 14 - i
+            tail, mine = arrived[dev + 1, 128:136], arrived[dev, 128:136]
+            whole, joins = tail[2:3] == tail[3:4], mine[3:4] == tail[2:3]
             total = jnp.where(joins, arrived[dev + 1, 0:64] + jnp.where(whole, total, 0.0), 0.0)
-            small = jnp.where(joins, tail[0:1] + jnp.where(whole, small, 0.0), 0.0)
-            back[dev, 64:128] = total
-            back[dev, 129:130] = small
-            return total, small
-
-        none = (jnp.zeros((64, 128), F32), jnp.zeros((1, 128), F32))
+            back[dev, 0:64] = total
+            return total
+
+        self.wait_piece(0, 0)
         for dev in range(16):
             back[dev, 128:136] = jnp.zeros((8, 128), F32)
-        back[0, 0:64] = none[0]
-        back[15, 64:128] = none[0]
-        lax.fori_loop(1, 16, left, none)
+        back[0, 64:128] = none
+        lax.fori_loop(1, 16, left, (none, small_none))
+        lax.fori_loop(0, 15, right_small, small_none)
+        self.send(back, self.r.got, 1, 0)
+        self.wait_piece(0, 1)
+        back[15, 0:64] = none
         lax.fori_loop(0, 15, right, none)
-        self.send(back, self.r.got, 1)
+        self.send(back, self.r.got, 1, 1)
 
 
 class Gains:
@@ -329,7 +343,7 @@
     ("gain_sum", (2, 8, D), F32), ("gain_here", (8, 128), F32), ("gain_pack", (7, 8, 128), F32), ("gain_mid", (8, 128), F32), ("gain_seq", (15, 8, 128), F32),
 ]
 SEMS = [
-    ("load", pltpu.SemaphoreType.DMA((9,))), ("esem", pltpu.SemaphoreType.DMA((2, 3))), ("gsem", pltpu.SemaphoreType.DMA((3,))),
+    ("load", pltpu.SemaphoreType.DMA((9,))), ("esem", pltpu.SemaphoreType.DMA((2, 6))), ("gsem", pltpu.SemaphoreType.DMA((3,))),
     ("ssem", pltpu.SemaphoreType.DMA((11,))), ("rsem", pltpu.SemaphoreType.DMA((11, 6))), ("free", pltpu.SemaphoreType.REGULAR((11, 2))),
 ]
 ROW_DOWN, ROW_UP, ROW_O, ROW_Q, ROW_K, ROW_V = 0, 2048, 4096, 4608, 5120, 5632
@@ -450,7 +464,8 @@
     def take_slab(h, sb):
         for half in range(2):
             lanes = pl.ds(half * 128, 128)
-            sb[h, 0:128, lanes] = r.got[2 * h + half, 0:128].astype(BF16)
+            sb[h, 0:64, lanes] = r.got[2 * h + half, 64:128].astype(BF16)
+            sb[h, 64:128, lanes] = r.got[2 * h + half, 0:64].astype(BF16)
             sb[h, 128:144, lanes] = jnp.concatenate(
                 [r.got[2 * h + half, 128:136], jnp.zeros((8, 128), F32)], axis=0).astype(BF16)
 
@@ -531,13 +546,14 @@
         back = dot_nt(r.gup[j], r.wup[j])
 
         r.gmid[...] = back if j == 0 else r.gmid[...] + back
-        r.g[ROW_DOWN + j * 512:ROW_DOWN + (j + 1) * 512, :] = dot_tn(r.xb[j], r.cot[...])
+        block(ROW_DOWN + j * 512, dot_tn(r.xb[j], r.cot[...]))
+        block(ROW_UP + j * 512, dot(r.hidT[...], r.gup[j]))
         return c
 
     X, Y, Z = 0, 1, 2
     early = [
         Part(r, where, k, ROW_DOWN + 512 * k, 512, axes, ("o", "ic"), ("ic", "o"))
-        for k, axes in enumerate(((X, Y, Z), (Y, Z, X), (Z, X, Y), (Z, Y, X)))
+        for k, axes in enumerate(((X, Y, Z), (Y, X, Z), (X, Y, Z), (Y, X, Z)))
     ]
     up = [
         Part(r, where, 4, ROW_UP, 1024, (X, Y, Z), ("c", "oi"), ("oi", "c")),
@@ -545,15 +561,19 @@
         Part(r, where, 6, ROW_UP + 1536, 512, (Y, X, Z), ("c", "oi"), ("ic", "o")),
     ]
     branch = Part(r, where, 7, ROW_O, 512, (Z, X, Y), ("o", "ic"), ("ic", "o"))
+    query = Part(r, where, 8, ROW_Q, 512, (Z, Y, X), ("o", "ic"), ("ic", "o"))
     last = [
-        Part(r, where, 8, ROW_Q, 512, (X, Y, Z), ("o", "ic"), ("ic", "o")),
-        Part(r, where, 9, ROW_Q + 512, 512, (Y, Z, X), ("o", "ic"), ("ic", "o")),
-        Part(r, where, 10, ROW_Q + 1024, 512, (Z, X, Y), ("o", "ic"), ("ic", "o")),
+        Part(r, where, 9, ROW_K, 512, (X, Y, Z), ("o", "ic"), ("ic", "o")),
+        Part(r, where, 10, ROW_V, 512, (Y, X, Z), ("o", "ic"), ("ic", "o")),
     ]
 
-    for j in range(4):
+    def block(row, value):
+        r.g[row:row + 512, :] = value
+
+    r.hidT[...] = r.hid[...].T
+    for j, moves in enumerate((early[:1], early[:2] + up[:1], early[1:3] + up[:2], early[2:4] + up[1:3])):
         feed(j, 0)
-        tick(*early[max(j - 1, 0):j + 1])
+        tick(*moves)
 
     def add_gain(which, p):
         total = r.gain_sum[which]
@@ -573,7 +593,9 @@
         return c
 
     row_loop(64, second_back)
-    tick(early[3])
+    tick(early[3], up[2])
+    block(ROW_O, dot(r.attT[...], r.gb[...]))
+    tick(branch)
     r.acc[...] = dot_nt(r.wo[...], r.gb[...])
 
     def gates(h):
@@ -590,17 +612,9 @@
         return ends(r.gext[h, 0:64].astype(F32), one_f * gd, one_l * gd)
 
     head_loop(gates)
+    tick(branch)
     exchange = Exchange(r, 1, pack, seq)
     exchange.begin()
-
-    def block(row, value):
-        r.g[row:row + 512, :] = value
-
-    r.hidT[...] = r.hid[...].T
-    for j in range(4):
-        block(ROW_UP + j * 512, dot(r.hidT[...], r.gup[j]))
-    block(ROW_O, dot(r.attT[...], r.gb[...]))
-    tick(*up, branch)
 
     def map_back(h, gphi, phi, flat, which):
         p = (gphi.astype(BF16).astype(F32) * phi.astype(F32)).astype(BF16)
@@ -613,12 +627,11 @@
         map_back(h, gphi, r.phiq[h], r.qT, 0)
         r.acc2[pl.ds(pl.multiple_of(h * 64, 64), 64)] = dot(r.gext[h, 0:64], same(dot_nt(r.phiq[h], r.phik[h])))
 
-    head_loop(query_back, 0, 3)
-    tick(*up, branch)
-    head_loop(query_back, 3, 8)
+    head_loop(query_back)
     exchange.turn()
     tick(*early)
     block(ROW_Q, dot_nt(r.nT[...], r.gT[0]))
+    tick(query)
     r.acc[...] = dot(r.xb[0], r.wdown[0])
     for j in range(1, 4):
         r.acc[...] += dot(r.xb[j], r.wdown[j])
@@ -628,14 +641,16 @@
         return c
 
     row_loop(64, put_out)
+    tick(query)
 
     def key_local(h):
         gphi = dot(same(dot_tn(r.vext[h], r.gext[h])), r.phiq[h]).astype(BF16)
         r.xb[h // 2, :, pl.ds(pl.multiple_of(h % 2 * 256, 256), 256)] = gphi
 
     head_loop(key_local)
+    tick(*up, branch)
     exchange.wait()
-    tick(*early)
+    tick(*early, query)
 
     def key_back(h):
         take_slab(h, r.sb2)
@@ -646,11 +661,12 @@
         r.gT[2, rows] = (r.acc2[rows] + jnp.where(in_f, far[0:64], 0.0) + jnp.where(in_l, far[64:128], 0.0)).astype(BF16)
 
     head_loop(key_back, 0, 4)
-    tick(*up)
+    tick(*up, branch)
     head_loop(key_back, 4, 8)
     block(ROW_K, dot_nt(r.nT[...], r.gT[1]))
     block(ROW_V, dot_nt(r.nT[...], r.gT[2]))
     tick(*last)
+    tick(*early, query)
     r.acc2[...] = dot(r.wqkv[0], r.gT[0])
 
     def normed_back(i, c):
@@ -660,7 +676,7 @@
     lax.fori_loop(1, 3, normed_back, 0)
     r.acc[...] = r.acc2[...].T
     tick(*last)
-    tick(*early, *up, branch)
+    tick(*up, branch, query)
 
     def first_back(rows, c):
         gn = r.acc[rows, :].astype(BF16).astype(F32)
@@ -679,14 +695,13 @@
     gains = Gains(r, pack, seq)
     gains.begin()
     tick(*last)
-    tick(*up, branch)
+    tick(*early)
     tick(*last)
-    tick(*early, branch)
     gains.turn()
     tick(*last)
-    tick(*up)
+    tick(*up, branch, query)
     tick(*last)
-    for part in early + up + [branch] + last:
+    for part in early + up + [branch, query] + last:
         while part.step <= part.last:
             part.tick()
     total = gains.end()

time: 175 us -> 163 us (0.931)
  Pallas kernels: 173 us -> 162 us
    pallas_call x1, Pallas kernels: 168 us -> 157 us  [per_device(): pl.pallas_call(kernel, out_shape=(pltpu.VMEM((T, D), BF16), pltpu.VMEM((T...]
where the time goes in v5:
time: 163 us
  Pallas kernels  162 us (99%)
    pallas_call x1, Pallas kernels, per_device(): pl.pallas_call(kernel, out_shape=(pltpu.VMEM((T, D), BF16), pltpu.VMEM((T...  157 us
    pallas_call x1, Pallas kernels, per_device(): pl.pallas_call(store_kernel, out_shape=(low, low, f32(D, D), f32(D, D), f...  4.98 us

profile of v5, /device:TPU:1, one launch (start us, length us, event | category | flops | bytes accessed | tf_op | source)
XLA Modules:
  0.0 162.8 jit_solution(2451280634305660778)
XLA Ops:
  0.6 157.0 %shard_map.204 = (bf16[512,512]{1,0:T(8,128)(2,1)S(1)}, bf16[512,512]{1,0:T(8,128)(2,1)S(1)}, f32[6144,512]{1,0:T(8,128)S(1)}, f32[8,512]{1,0:T(8,128)S(1)}) custom-call(bf16[512,512]{1,0:T(8,128)(2,1)} %bitcast.8, bf16[512,512]{1,0:T(8,128)(2,1)} %wq_h.1, bf16[512,512]{1,0:T(8,128)(2,1)} %wk_h.1, bf16[512,512]{1,0:T(8,128)(2,1)} %wv_h.1, ...), custom_call_target="tpu_custom_call" | custom-call | tf_op jit(solution)/shard_map/pallas_call | solution.py:731
  157.7 5.0 %shard_map.205 = (bf16[512,512]{1,0:T(8,128)(2,1)}, bf16[512,512]{1,0:T(8,128)(2,1)}, f32[512,512]{1,0:T(8,128)}, f32[512,512]{1,0:T(8,128)}, f32[512,512]{1,0:T...) custom-call(bf16[512,512]{1,0:T(8,128)(2,1)S(1)} %get-tuple-element., ...), custom_call_target="tpu_custom_call" | custom-call | tf_op jit(solution)/shard_map/pallas_call | solution.py:742

commit v6 on v5

--- a/solution.py
+++ b/solution.py
@@ -13,7 +13,7 @@
 T, D, H, DH, M, FF = 512, 512, 8, 64, 256, 2048
 SLAB = 136
 EPS = 1e-05
-VMEM_LIMIT = 47 * 2**20
+VMEM_LIMIT = 50 * 2**20
 C = DH ** -0.25
 ALPHA = C * math.log2(math.e)
 GELU_A, GELU_B = math.sqrt(2.0 / math.pi), 0.044715
@@ -54,7 +54,7 @@
     def run(i, c):
         return body(pl.ds(pl.multiple_of(i * step, step), step), c)
 
-    return lax.fori_loop(0, T // step, run, carry)
+    return lax.fori_loop(0, T // step, run, carry, unroll=2)
 
 
 def head_loop(body, start=0, stop=H):
@@ -62,7 +62,7 @@
         body(h)
         return c
 
-    lax.fori_loop(start, stop, run, 0)
+    lax.fori_loop(start, stop, run, 0, unroll=4 if (stop - start) % 4 == 0 else 2)
 
 
 def wait_all(like, send_sem, recv_sem, dev):
@@ -542,7 +542,7 @@
             r.gup[j, rows, :] = (ga * slope).astype(BF16)
             return c
 
-        row_loop(16, gelu)
+        row_loop(32, gelu)
         back = dot_nt(r.gup[j], r.wup[j])
 
         r.gmid[...] = back if j == 0 else r.gmid[...] + back
@@ -666,7 +666,7 @@
     block(ROW_K, dot_nt(r.nT[...], r.gT[1]))
     block(ROW_V, dot_nt(r.nT[...], r.gT[2]))
     tick(*last)
-    tick(*early, query)
+    tick(*early, up[0], branch, query)
     r.acc2[...] = dot(r.wqkv[0], r.gT[0])
 
     def normed_back(i, c):
@@ -676,7 +676,6 @@
     lax.fori_loop(1, 3, normed_back, 0)
     r.acc[...] = r.acc2[...].T
     tick(*last)
-    tick(*up, branch, query)
 
     def first_back(rows, c):
         gn = r.acc[rows, :].astype(BF16).astype(F32)
@@ -697,9 +696,10 @@
     tick(*last)
     tick(*early)
     tick(*last)
+    tick(*up[1:], query)
     gains.turn()
     tick(*last)
-    tick(*up, branch, query)
+    tick(up[0], branch, *up[1:], query)
     tick(*last)
     for part in early + up + [branch, query] + last:
         while part.step <= part.last:

time: 163 us -> 158 us (0.969)
  Pallas kernels: 162 us -> 157 us
    pallas_call x1, Pallas kernels: 157 us -> 152 us  [per_device(): pl.pallas_call(kernel, out_shape=(pltpu.VMEM((T, D), BF16), pltpu.VMEM((T...]
where the time goes in v6:
time: 158 us
  Pallas kernels  157 us (99%)
    pallas_call x1, Pallas kernels, per_device(): pl.pallas_call(kernel, out_shape=(pltpu.VMEM((T, D), BF16), pltpu.VMEM((T...  152 us
    pallas_call x1, Pallas kernels, per_device(): pl.pallas_call(store_kernel, out_shape=(low, low, f32(D, D), f32(D, D), f...  4.98 us

profile of v6, /device:TPU:1, one launch (start us, length us, event | category | flops | bytes accessed | tf_op | source)
XLA Modules:
  0.0 157.6 jit_solution(5760577150418671633)
XLA Ops:
  0.6 151.8 %shard_map.204 = (bf16[512,512]{1,0:T(8,128)(2,1)S(1)}, bf16[512,512]{1,0:T(8,128)(2,1)S(1)}, f32[6144,512]{1,0:T(8,128)S(1)}, f32[8,512]{1,0:T(8,128)S(1)}) custom-call(bf16[512,512]{1,0:T(8,128)(2,1)} %bitcast.8, bf16[512,512]{1,0:T(8,128)(2,1)} %wq_h.1, bf16[512,512]{1,0:T(8,128)(2,1)} %wk_h.1, bf16[512,512]{1,0:T(8,128)(2,1)} %wv_h.1, ...), custom_call_target="tpu_custom_call" | custom-call | tf_op jit(solution)/shard_map/pallas_call | solution.py:731
  152.5 5.0 %shard_map.205 = (bf16[512,512]{1,0:T(8,128)(2,1)}, bf16[512,512]{1,0:T(8,128)(2,1)}, f32[512,512]{1,0:T(8,128)}, f32[512,512]{1,0:T(8,128)}, f32[512,512]{1,0:T...) custom-call(bf16[512,512]{1,0:T(8,128)(2,1)S(1)} %get-tuple-element., ...), custom_call_target="tpu_custom_call" | custom-call | tf_op jit(solution)/shard_map/pallas_call | solution.py:742

commit v7 on v6

--- a/solution.py
+++ b/solution.py
@@ -391,9 +391,6 @@
         return jnp.concatenate(
             [jnp.where(in_f, block, zero).astype(BF16), jnp.where(in_l, block, zero).astype(BF16), tail.astype(BF16)], axis=0)
 
-    dcol = jnp.broadcast_to(doc, (128, T)).T
-    for j in range(4):
-        r.dcol[:, j * 128:(j + 1) * 128] = dcol
     live = jnp.broadcast_to(live_ref[...].astype(F32), (128, T)).T
 
     loads["x"].wait()
@@ -411,14 +408,12 @@
         r.rx[p] = jnp.where(pick, 1.0, 0.0).astype(BF16)
         r.rx[p, 0:64, 0:256] = r.rf[2 * p]
         r.rx[p, 64:128, 256:512] = r.rf[2 * p + 1]
-    for h in range(H):
-        r.r80[h, 0:64] = r.rf[h]
-        r.r80[h, 64:80] = jnp.where(iota((16, M), 0) == 0, 1.0, 0.0).astype(BF16)
     pick_heads = ((iota((D, 128), 1) % 8 == iota((D, 128), 0) // DH) & (iota((D, 128), 1) < 24)).astype(BF16)
 
     def features(w, low, transposed, phi, off, alive):
         flat = dot(r.nb[...], r.wqkv[w]).astype(BF16)
-        transposed[...] = flat.T
+        if transposed is not None:
+            transposed[...] = flat.T
         square = flat.astype(F32)
         square = square * square
         high = square.astype(BF16)
@@ -446,7 +441,7 @@
         lax.fori_loop(0, 4, one_pair, 0)
 
     loads["wk"].wait()
-    features(1, r.xb, r.kT, r.phik, 0, live)
+    features(1, r.xb, None, r.phik, 0, live)
     loads["wv"].wait()
     vT = dot(r.nb[...], r.wqkv[2]).astype(BF16).T
     for h in range(H):
@@ -483,6 +478,14 @@
         pltpu.make_async_copy(wdown_h.at[pl.ds(j * 512, 512)], r.wdown.at[j], r.load.at[8]).start()
 
     r.nT[...] = r.nb[...].T
+    dcol = jnp.broadcast_to(doc, (128, T)).T
+    for j in range(4):
+        r.dcol[:, j * 128:(j + 1) * 128] = dcol
+    for h in range(H):
+        r.r80[h, 0:64] = r.rf[h]
+        r.r80[h, 64:80] = jnp.where(iota((16, M), 0) == 0, 1.0, 0.0).astype(BF16)
+    for p in range(4):
+        r.kT[p * 128:(p + 1) * 128] = r.xb[p, :, 0:128].T
     loads["wq"].wait()
     features(0, r.xb, r.qT, r.phiq, 256, None)
     exchange.turn()

time: 158 us -> 160 us (1.013)
  Pallas kernels: 157 us -> 159 us
    pallas_call x1, Pallas kernels: 152 us -> 154 us  [per_device(): pl.pallas_call(kernel, out_shape=(pltpu.VMEM((T, D), BF16), pltpu.VMEM((T...]
where the time goes in v7:
time: 160 us
  Pallas kernels  159 us (99%)
    pallas_call x1, Pallas kernels, per_device(): pl.pallas_call(kernel, out_shape=(pltpu.VMEM((T, D), BF16), pltpu.VMEM((T...  154 us
    pallas_call x1, Pallas kernels, per_device(): pl.pallas_call(store_kernel, out_shape=(low, low, f32(D, D), f32(D, D), f...  4.98 us

profile of v7, /device:TPU:1, one launch (start us, length us, event | category | flops | bytes accessed | tf_op | source)
XLA Modules:
  0.0 159.6 jit_solution(6086384265187043392)
XLA Ops:
  0.6 153.8 %shard_map.204 = (bf16[512,512]{1,0:T(8,128)(2,1)S(1)}, bf16[512,512]{1,0:T(8,128)(2,1)S(1)}, f32[6144,512]{1,0:T(8,128)S(1)}, f32[8,512]{1,0:T(8,128)S(1)}) custom-call(bf16[512,512]{1,0:T(8,128)(2,1)} %bitcast.8, bf16[512,512]{1,0:T(8,128)(2,1)} %wq_h.1, bf16[512,512]{1,0:T(8,128)(2,1)} %wk_h.1, bf16[512,512]{1,0:T(8,128)(2,1)} %wv_h.1, ...), custom_call_target="tpu_custom_call" | custom-call | tf_op jit(solution)/shard_map/pallas_call | solution.py:734
  154.5 5.0 %shard_map.205 = (bf16[512,512]{1,0:T(8,128)(2,1)}, bf16[512,512]{1,0:T(8,128)(2,1)}, f32[512,512]{1,0:T(8,128)}, f32[512,512]{1,0:T(8,128)}, f32[512,512]{1,0:T...) custom-call(bf16[512,512]{1,0:T(8,128)(2,1)S(1)} %get-tuple-element., ...), custom_call_target="tpu_custom_call" | custom-call | tf_op jit(solution)/shard_map/pallas_call | solution.py:745
